TPU v7x, 128 devices: a whole 4x4x4 slice. The times are simulated.
128 devices in a mesh: param: 8 (over y, z_hi), obs: 16 (over x, z_lo, core).
Axes of the slice: x: 4, y: 4, z: 4 (z_hi: 2, z_lo: 2; z = z_hi * 2 + z_lo), core: 2. Of those that a mesh axis runs over, the one named last changes fastest.
Arguments:
- design: bfloat16 [10240, 8192], P('obs', 'param'), may hold values from -6 to 6
- observed: bfloat16 [10240], P('obs'), may hold values from -6 to 6
- row_weight: float32 [10240], P('obs'), may hold values from 0.3 to 3
- taps: float32 [7], replicated, may hold values from -0.5 to 0.5
Outputs:
- normal: float32 [8192, 8192], P('obs', 'param')
- rhs: float32 [8192], P('param')
- filtered_obs: float32 [10240], P('obs')
All inputs are finite; a program needn't handle non-finite values.
Results may differ from a plain program's by a relative error of at most 0.0035.
Values may be sent and summed in bfloat16 or wider, within the bound.
A program may use at most 128 MiB of HBM per device.

v0:
```python
import math

import jax
import jax.numpy as jnp
from jax import lax
from jax.sharding import PartitionSpec as P


def passed_along(value, axis, steps):
    count = lax.axis_size(axis)
    first, last = (max(0, -steps), min(count, count - steps))
    return lax.ppermute(value, axis, [(source, source + steps) for source in range(first, last)])


def apply_filter(values, earlier_rows, taps):
    lags = taps.shape[0]
    count = values.shape[0]
    joined = jnp.concatenate([earlier_rows, values], 0).astype(jnp.float32)
    total = joined[lags:]
    for lag in range(1, lags + 1):
        total = total + taps[lag - 1] * joined[lags - lag : lags - lag + count]
    return total


def per_device(design, observed, row_weight, taps):
    lags = taps.shape[0]
    tails = passed_along((design[-lags:], observed[-lags:]), "obs", 1)
    filtered = apply_filter(design, tails[0], taps).astype(jnp.bfloat16)
    filtered_obs = apply_filter(observed, tails[1], taps)
    n_obs = lax.axis_size("obs")
    total_rows = filtered.shape[0] * n_obs
    weighted_obs = (row_weight * filtered_obs).astype(jnp.bfloat16)
    partial_rhs = jnp.dot(weighted_obs, filtered, preferred_element_type=jnp.float32)
    rhs = lax.psum(partial_rhs, "obs") / math.sqrt(total_rows)
    contract = (((0,), (0,)), ((), ()))
    weighted = (row_weight[:, None] * filtered.astype(jnp.float32)).astype(jnp.bfloat16)
    gathered = lax.all_gather(filtered, "param", axis=1, tiled=True)
    normal = (
        lax.psum_scatter(
            lax.dot_general(gathered, weighted, contract, preferred_element_type=jnp.float32),
            "obs",
            scatter_dimension=0,
            tiled=True,
        )
        / total_rows
    )
    return (normal, rhs, filtered_obs)


def solution(mesh):
    placed = (P("obs", "param"), P("obs"), P("obs"), P())
    return jax.shard_map(
        per_device,
        mesh=mesh,
        in_specs=placed,
        out_specs=(P("obs", "param"), P("param"), P("obs")),
        check_vma=False,
    )
```

profile of v0, /device:TPU:34, one launch (start us, length us, event | category | flops | bytes accessed | tf_op | source)
XLA Modules:
  0.0 533.4 jit_solution(17220770275866772690)
XLA Ops:
  7.2 0.0 all-gather.2.cloned.1.call-start
  7.2 0.7 slice.82
  7.9 1.9 collective-permute-start
  9.9 1.6 fusion.10
  11.4 1.5 collective-permute-done
  13.0 1.7 maximum_convert_fusion
  14.7 0.0 copy-start.1
  14.7 7.6 %fusion.1 = bf16[640,1024]{1,0:T(8,128)(2,1)} fusion(f32[647,1024]{1,0:T(8,128)S(1)} %maximum_convert_fusion, f32[]{:T(128)} %bitcast.6, f32[]{:T(128)} %bitcast.5, f32[]{:T(128)} %bitcast.4, f32[]{:T(128)} %bitcast.3, f32[]{:T(128)} %bitcast.2, f32[]{:T(128)} %bitcast.1, f32[]{:T(128)} %bitcast), kind=kLoop, calls=%fused_computation.2 | loop fusion | flops 9830400 | bytes 22282268 | tf_op jit(solution)/shard_map/convert_element_type | solution.py:28
  22.3 0.0 all-gather.2.cloned.1.call-update
  22.3 0.0 reduce-scatter.2.cloned.1.call-start
  22.4 130.2 %all-gather.2.cloned.1.call-done = bf16[640,8192]{1,0:T(8,128)(2,1)} async-done(((bf16[640,1024]{1,0:T(8,128)(2,1)}), bf16[640,8192]{1,0:T(8,128)(2,1)}) %all-gather.2.cloned.1.call-update) | async-done | bytes 10485776 | tf_op jit(solution)/shard_map/all_gather | solution.py:37
  152.5 22.3 %fusion.8 = f32[8192,1024]{1,0:T(8,128)} fusion(bf16[640,8192]{1,0:T(8,128)(2,1)} %all-gather.2.cloned.1.call-done, bf16[640,1024]{1,0:T(8,128)(2,1)} %fusion.1, f32[640]{0:T(1024)S(1)} %copy-done.1), kind=kOutput, calls=%fused_computation.17 | convolution fusion | flops 10739384320 | bytes 45353472 | tf_op jit(solution)/shard_map/dot_general | solution.py:40
  174.8 0.0 reduce-scatter.2.cloned.1.call-update
  174.9 0.7 copy-done.2
  175.5 0.1 slice.98
  175.6 1.9 collective-permute-start.1
  177.5 2.9 collective-permute-done.1
  180.4 0.1 maximum_convert_fusion.1
  180.5 5.0 multiply_convert_fusion.2
  185.5 0.3 fusion.11
  185.8 33.3 %psum.7 = f32[1024]{0:T(1024)S(1)} all-reduce(f32[1024]{0:T(1024)S(1)} %bitcast.11), channel_id=1, replica_groups=mesh['param'=8,'obs'=16] {'obs'}, use_global_device_ids=true, to_apply=%region_1.0 | all-reduce | flops 1024 | bytes 8192 | tf_op jit(solution)/shard_map/psum | solution.py:34
  219.2 0.6 broadcast_multiply_fusion.1
  219.8 303.5 %reduce-scatter.2.cloned.1.call-done = f32[512,1024]{1,0:T(8,128)} async-done(((f32[8192,1024]{1,0:T(8,128)}), f32[512,1024]{1,0:T(8,128)}) %reduce-scatter.2.cloned.1.call-update) | async-done | bytes 2097168 | tf_op jit(solution)/shard_map/reduce_scatter | solution.py:39
  523.2 3.3 broadcast_multiply_fusion
  (5 shorter events, 0.0 us)
Async XLA Ops:
  7.2 145.4 %all-gather.2.cloned.1.call-start = ((), (), s32[]{:S(2)}) async-start(), calls=%async_computation.1 | async-start | bytes 11796480 | tf_op jit(solution)/shard_map/all_gather | solution.py:37
  7.9 5.0 collective-permute-start
  14.7 137.9 %copy-start.1 = (f32[640]{0:T(1024)S(1)}, f32[640]{0:T(1024)}, u32[]{:S(2)}) copy-start(f32[640]{0:T(1024)} %param.6) | copy-start | bytes 7684
  22.3 500.9 %reduce-scatter.2.cloned.1.call-start = ((), (), s32[]{:S(2)}) async-start(), calls=%async_computation.2 | async-start | bytes 35651584 | tf_op jit(solution)/shard_map/reduce_scatter | solution.py:39
  174.8 0.7 copy-start.2
  174.8 10.7 %copy-start = (bf16[640,1024]{1,0:T(8,128)(2,1)S(1)}, bf16[640,1024]{1,0:T(8,128)(2,1)}, u32[]{:S(2)}) copy-start(bf16[640,1024]{1,0:T(8,128)(2,1)} %fusion.1) | copy-start | bytes 3932164
  175.6 4.8 collective-permute-start.1
Sparse Core Ops, SparseCore 0:
  22.5 130.0 all-gather.1
  175.0 348.1 reduce-scatter.1
where the time goes:
time: 535 us; the launch traced here: 533 us
  waiting for transfers between devices  438 us (82%)
  blocking collectives  33.3 us (6%)
  matrix products  22.6 us (4%)
  other arithmetic  18.3 us (3%)
  between operations  14.1 us (3%)
    reduce_scatter x1, waiting for transfers between devices, per_device(): lax.psum_scatter(lax.dot_general(gathered, weighted, contract, preferred_...  303 us
    all_gather x1, waiting for transfers between devices, per_device(): gathered = lax.all_gather(filtered, 'param', axis=1, tiled=True)  130 us
    psum x1, blocking collectives, per_device(): rhs = lax.psum(partial_rhs, 'obs') / math.sqrt(total_rows)  33.3 us
    dot_general x1, matrix products, per_device(): lax.dot_general(gathered, weighted, contract, preferred_element_type=jnp....  22.3 us
  transfers between devices with their start and end apart: 4, of which 4 were waited for; matrix products, arithmetic and copies ran while one was open for 1% of the time, Pallas kernels for 0%

commit v1 on v0

v1 whole, which is shorter than its diff:
```python
import functools
import math

import jax
import jax.numpy as jnp
from jax import lax
from jax.experimental import pallas as pl
from jax.experimental.pallas import tpu as pltpu
from jax.sharding import PartitionSpec as P

MESH = pl.DeviceIdType.MESH
BF16, F32 = jnp.bfloat16, jnp.float32
ROWS = 640
COLS = 1024
LAGS = 7
PART = 256
DEPTH = 2 * ROWS


def kernel(
    scale, rhs_scale,
    design, observed, weight, taps,
    normal, rhs, filtered_obs,
    ext, halo, obs_tail, obs_halo, wcol, sent, weighted, rows, cols, part, own, from_left, from_right, far_left, far_right,
    leaving, landed, rhs_all,
    halo_s, halo_r, rows_s, rows_f, rows_sib, rows_r, cols_s, cols_sib, cols_f, cols_r, x_s, x_r, z_s, z_r, rhs_s, rhs_r,
):
    p, o = lax.axis_index("param"), lax.axis_index("obs")
    y, h = p // 2, p % 2
    x, l, k = o // 4, (o // 2) % 2, o % 2
    near = (y - x + 4) % 4
    settled = l == h

    def param_of(y_, h_):
        return ((y_ + 4) % 4) * 2 + h_

    def obs_of(x_, l_, k_):
        return ((x_ + 4) % 4) * 4 + l_ * 2 + k_

    sibling = (p, obs_of(x, l, 1 - k))
    up = [(param_of(y + 1, h), obs_of(x, l, k)), (param_of(y + 1, h), obs_of(x, l, 1 - k))]
    down = [(param_of(y - 1, h), obs_of(x, l, k)), (param_of(y - 1, h), obs_of(x, l, 1 - k))]
    right, left = (p, obs_of(x + 1, l, k)), (p, obs_of(x - 1, l, k))
    across = (param_of(y, 1 - h), o)
    beside = (p, obs_of(x, 1 - l, k))
    corner = (param_of(y, 1 - h), obs_of(x, 1 - l, k))
    following = (p, (o + 1) % 16)

    def remote(src, dst, send, recv, device):
        return pltpu.make_async_remote_copy(
            src_ref=src, dst_ref=dst, send_sem=send, recv_sem=recv, device_id=device, device_id_type=MESH
        )

    def halo_copies():
        return (
            remote(design.at[pl.ds(ROWS - 16, 16), :], halo, halo_s.at[0], halo_r.at[0], following),
            remote(obs_tail, obs_halo, halo_s.at[1], halo_r.at[1], following),
        )

    def own_piece(m, rel):
        return rows.at[0, m, :, pl.ds(0, ROWS)] if rel == 0 else sent.at[m]

    def lanes(rel):
        return pl.ds(ROWS * rel, ROWS)

    def rows_up(m, rel):
        return remote(own_piece(m, rel), rows.at[3, m, :, lanes(rel)], rows_s.at[0, m, rel], rows_r.at[3, m, rel], up[rel])

    def rows_down(m, rel):
        return remote(own_piece(m, rel), rows.at[1, m, :, lanes(rel)], rows_s.at[1, m, rel], rows_r.at[1, m, rel], down[rel])

    def rows_on(m, rel):
        source = rows.at[3 if m == 0 else 1, m, :, lanes(rel)]
        return remote(
            source, rows.at[2, m, :, lanes(rel)], rows_f.at[m, rel], rows_r.at[2, m, rel], up[0] if m == 0 else down[0]
        )

    def rows_over(m):
        return remote(sent.at[m], rows.at[0, m, :, lanes(1)], rows_sib.at[m], rows_r.at[0, m, 1], sibling)

    def cols_over(n):
        half = pl.ds(0, ROWS)
        return remote(cols.at[0, n, half, :], cols.at[0, n, pl.ds(ROWS, ROWS), :], cols_sib.at[n], cols_r.at[0, n, 1], sibling)

    def cols_across(n):
        half = pl.ds(0, ROWS)
        return remote(cols.at[0, n, half, :], cols.at[1, n, half, :], cols_s.at[n], cols_r.at[1, n, 0], across)

    def cols_on(n):
        half = pl.ds(0, ROWS)
        return remote(cols.at[1, n, half, :], cols.at[1, n, pl.ds(ROWS, ROWS), :], cols_f.at[n], cols_r.at[1, n, 1], sibling)

    def x_far(d, hr):
        dst = (far_left if d == 0 else far_right).at[hr]
        return remote(part.at[1, d, hr], dst, x_s.at[d, 0, hr], x_r.at[d, 0, hr], right if d == 0 else left)

    def x_raw(d, hr):
        m = 1 - d
        dst = (from_left if d == 0 else from_right).at[m, hr]
        return remote(part.at[0 if d == 0 else 2, m, hr], dst, x_s.at[d, 1, hr], x_r.at[d, 1, hr], right if d == 0 else left)

    def x_sum(d, hr):
        m = d
        dst = (from_left if d == 0 else from_right).at[m, hr]
        return remote(part.at[0 if d == 0 else 2, m, hr], dst, x_s.at[d, 2, hr], x_r.at[d, 2, hr], right if d == 0 else left)

    def z_beside(m):
        return remote(leaving.at[0, m], landed.at[0, m], z_s.at[0, m], z_r.at[0, m], beside)

    def z_across(m):
        return remote(leaving.at[1, m], landed.at[0, m], z_s.at[1, m], z_r.at[0, m], across)

    def z_corner(m):
        return remote(leaving.at[1, m], landed.at[1, m], z_s.at[1, m], z_r.at[1, m], corner)

    def rhs_to(step):
        peer = (p, (o + step) % 16)
        return remote(rhs_all.at[o], rhs_all.at[o], rhs_s.at[step], rhs_r.at[step], peer)

    barrier = pltpu.get_barrier_semaphore()
    greeted = up + down + [across, corner] + [(p, (o + step) % 16) for step in range(1, 16)]
    for device in greeted:
        pl.semaphore_signal(barrier, inc=1, device_id=device, device_id_type=MESH)

    signal_row = jnp.broadcast_to(observed[...].astype(F32), (8, ROWS))
    weight_row = jnp.broadcast_to(weight[...], (8, ROWS))
    obs_tail[...] = signal_row[:, ROWS - 128 :]
    for r in range(ROWS // 128):
        block = jnp.broadcast_to(weight[:, r * 128 : (r + 1) * 128], (128, 128))
        wcol[pl.ds(r * 128, 128), :] = block.T

    def widen(i, _):
        at = pl.multiple_of(i * 128, 128)
        ext[pl.ds(8, ROWS), pl.ds(at, 128)] = design[:, pl.ds(at, 128)].astype(F32)
        return 0

    lax.fori_loop(0, COLS // 128, widen, 0)
    pl.semaphore_wait(barrier, len(greeted))

    @pl.when(o < 15)
    def _():
        for copy in halo_copies():
            copy.start()

    @pl.when(o > 0)
    def _():
        for copy in halo_copies():
            copy.wait_recv()
        ext[pl.ds(0, 8), :] = halo[...].astype(F32)[8:]

    @pl.when(o == 0)
    def _():
        ext[pl.ds(0, 8), :] = jnp.zeros((8, COLS), F32)
        obs_halo[...] = jnp.zeros((8, 128), F32)

    def filter_piece(m, rel):
        core = k if rel == 0 else 1 - k

        def block(c, _):
            within = pl.multiple_of(c * 128, 128)
            at = pl.multiple_of(core * 512 + m * PART + within, 128)
            for r in range(ROWS // 128):
                first = r * 128
                total = ext[pl.ds(8 + first, 128), pl.ds(at, 128)]
                for lag in range(1, LAGS + 1):
                    total = total + taps[lag - 1] * ext[pl.ds(8 + first - lag, 128), pl.ds(at, 128)]
                rounded = total.astype(BF16).astype(F32)
                scaled = (wcol[pl.ds(first, 128), :] * rounded).astype(BF16)
                cols[0, core, pl.ds(first, 128), pl.ds(pl.multiple_of(m * PART + within, 128), 128)] = scaled
                turned = rounded.T.astype(BF16)
                if rel == 0:
                    rows[0, m, pl.ds(within, 128), pl.ds(first, 128)] = turned
                else:
                    sent[m, pl.ds(within, 128), pl.ds(first, 128)] = turned
            return 0

        lax.fori_loop(0, PART // 128, block, 0)

    first_far = near == 2
    for m in range(2):
        for rel in (1, 0):
            filter_piece(m, rel)
            (rows_up if m == 0 else rows_down)(m, rel).start()
            if rel == 1:
                rows_over(m).start()
    for n in range(2):
        cols_over(n).start()
        cols_across(n).start()

    @pl.when(first_far)
    def _():
        for rel in (1, 0):
            rows_up(1, rel).start()
            rows_down(0, rel).start()

    extended = jnp.concatenate([obs_halo[...], signal_row], axis=1)
    total = signal_row
    for lag in range(1, LAGS + 1):
        total = total + taps[lag - 1] * pltpu.roll(extended, lag, 1)[:, 128:]
    filtered_obs[...] = total[0:1, :]
    weighted[...] = jnp.concatenate([weight_row * total, weight_row * total], axis=0).astype(BF16)
    line = lax.broadcasted_iota(jnp.int32, (8, 128), 0)
    sums = jnp.zeros((8, 128), F32)
    for m in range(2):
        for rel in range(2):
            core = k if rel == 0 else 1 - k
            piece = rows[0, m, :, pl.ds(0, ROWS)] if rel == 0 else sent[m]
            dots = lax.dot_general(weighted[...], piece, (((1,), (1,)), ((), ())), preferred_element_type=F32)
            for c in range(2):
                sums = jnp.where(line == core * 4 + m * 2 + c, dots[0:8, c * 128 : (c + 1) * 128], sums)
    rhs_all[o] = sums
    for step in range(1, 16):
        rhs_to(step).start()

    def multiply(dy, m, hr):
        role = (near + dy) % 4

        def chunk(c, _):
            at = pl.multiple_of((c % 2) * 256, 256)
            value = jnp.dot(rows[dy, m], cols[hr, c // 2, :, pl.ds(at, 256)], preferred_element_type=F32)
            to = pl.ds(pl.multiple_of(c * 256, 256), 256)

            @pl.when(role == 0)
            def _():
                own[m, hr, :, to] = value

            @pl.when(role != 0)
            def _():
                part[role - 1, m, hr, :, to] = value.astype(BF16)

            return 0

        lax.fori_loop(0, COLS // 256, chunk, 0)

        @pl.when(role == 2)
        def _():
            x_far(m, hr).start()

        @pl.when(role == (1 if m == 1 else 3))
        def _():
            x_raw(1 - m, hr).start()

    for m in range(2):
        rows_over(m).wait_recv()
        cols_over(m).wait_recv()
    for m in range(2):
        multiply(0, m, 0)

    for rel in (1, 0):
        rows_up(0, rel).wait_recv()
        rows_on(0, rel).start()
        rows_down(1, rel).wait_recv()
        rows_on(1, rel).start()

    @pl.when(jnp.logical_not(first_far))
    def _():
        for rel in (1, 0):
            rows_up(1, rel).start()
            rows_down(0, rel).start()

    multiply(3, 0, 0)
    multiply(1, 1, 0)
    for n in range(2):
        cols_across(n).wait_recv()
        cols_on(n).start()
    for n in range(2):
        cols_on(n).wait_recv()
    for m in range(2):
        multiply(0, m, 1)
    multiply(3, 0, 1)
    multiply(1, 1, 1)
    for m in range(2):
        for rel in range(2):
            rows_on(m, rel).wait_recv()
    for hr in range(2):
        for m in range(2):
            multiply(2, m, hr)
    for rel in range(2):
        rows_up(1, rel).wait_recv()
        rows_down(0, rel).wait_recv()
    for hr in range(2):
        multiply(1, 0, hr)
        multiply(3, 1, hr)

    for hr in range(2):
        for d in range(2):
            x_far(d, hr).wait_recv()
            at = 0 if d == 0 else 2
            gained = (far_left if d == 0 else far_right)[hr]
            part[at, d, hr] = (part[at, d, hr].astype(F32) + gained.astype(F32)).astype(BF16)
            x_sum(d, hr).start()

    for step in range(1, 16):
        rhs_to(step).wait_recv()
    total = rhs_all[0]
    for step in range(1, 16):
        total = total + rhs_all[step]
    rhs[...] = total * rhs_scale

    for hr in range(2):
        for m in range(2):
            (x_sum if m == 0 else x_raw)(0, hr).wait_recv()
            (x_sum if m == 1 else x_raw)(1, hr).wait_recv()
            total = own[m, hr] + from_left[m, hr].astype(F32) + from_right[m, hr].astype(F32)
            if hr == 0:

                @pl.when(settled)
                def _():
                    own[m, 0] = total

                @pl.when(jnp.logical_not(settled))
                def _():
                    leaving[0, m] = total.astype(BF16)
                    z_beside(m).start()

            else:
                leaving[1, m] = total.astype(BF16)

                @pl.when(settled)
                def _():
                    z_across(m).start()

                @pl.when(jnp.logical_not(settled))
                def _():
                    z_corner(m).start()

    for m in range(2):
        z_across(m).wait_recv()
        at = pl.ds(m * PART, PART)

        @pl.when(settled)
        def _():
            normal[at, :] = (own[m, 0] + landed[0, m].astype(F32)) * scale

        @pl.when(jnp.logical_not(settled))
        def _():
            z_corner(m).wait_recv()
            normal[at, :] = (landed[0, m].astype(F32) + landed[1, m].astype(F32)) * scale

    @pl.when(o < 15)
    def _():
        for copy in halo_copies():
            copy.wait_send()

    for m in range(2):
        rows_over(m).wait_send()
        cols_over(m).wait_send()
        cols_across(m).wait_send()
        cols_on(m).wait_send()
        z_across(m).wait_send()

        @pl.when(jnp.logical_not(settled))
        def _():
            z_beside(m).wait_send()

        for rel in range(2):
            rows_up(m, rel).wait_send()
            rows_down(m, rel).wait_send()
            rows_on(m, rel).wait_send()
        for d in range(2):
            x_far(d, m).wait_send()
            x_raw(d, m).wait_send()
            x_sum(d, m).wait_send()
    for step in range(1, 16):
        rhs_to(step).wait_send()


def per_device(design, observed, row_weight, taps):
    total_rows = ROWS * lax.axis_size("obs")
    dma = pltpu.SemaphoreType.DMA
    vmem = pl.BlockSpec(memory_space=pltpu.VMEM)
    normal, rhs, filtered_obs = pl.pallas_call(
        functools.partial(kernel, 1.0 / total_rows, 1.0 / math.sqrt(total_rows)),
        out_shape=(
            jax.ShapeDtypeStruct((512, COLS), F32),
            jax.ShapeDtypeStruct((8, 128), F32),
            jax.ShapeDtypeStruct((1, ROWS), F32),
        ),
        in_specs=[vmem, vmem, vmem, pl.BlockSpec(memory_space=pltpu.SMEM)],
        out_specs=(vmem, vmem, vmem),
        scratch_shapes=[
            pltpu.VMEM((ROWS + 8, COLS), F32),
            pltpu.VMEM((16, COLS), BF16),
            pltpu.VMEM((8, 128), F32),
            pltpu.VMEM((8, 128), F32),
            pltpu.VMEM((ROWS, 128), F32),
            pltpu.VMEM((2, PART, ROWS), BF16),
            pltpu.VMEM((16, ROWS), BF16),
            pltpu.VMEM((4, 2, PART, DEPTH), BF16),
            pltpu.VMEM((2, 2, DEPTH, 512), BF16),
            pltpu.VMEM((3, 2, 2, PART, COLS), BF16),
            pltpu.VMEM((2, 2, PART, COLS), F32),
            pltpu.VMEM((2, 2, PART, COLS), BF16),
            pltpu.VMEM((2, 2, PART, COLS), BF16),
            pltpu.VMEM((2, PART, COLS), BF16),
            pltpu.VMEM((2, PART, COLS), BF16),
            pltpu.VMEM((2, 2, PART, COLS), BF16),
            pltpu.VMEM((2, 2, PART, COLS), BF16),
            pltpu.VMEM((16, 8, 128), F32),
            dma((2,)), dma((2,)),
            dma((2, 2, 2)), dma((2, 2)), dma((2,)), dma((4, 2, 2)),
            dma((2,)), dma((2,)), dma((2,)), dma((2, 2, 2)),
            dma((2, 3, 2)), dma((2, 3, 2)),
            dma((2, 2)), dma((2, 2)),
            dma((16,)), dma((16,)),
        ],
        compiler_params=pltpu.CompilerParams(collective_id=0, has_side_effects=True, vmem_limit_bytes=60 << 20),
        name="normal_equations",
    )(design, observed.reshape(1, ROWS), row_weight.reshape(1, ROWS), taps)
    return normal, rhs.reshape(COLS), filtered_obs.reshape(ROWS)


def solution(mesh):
    placed = (P("obs", "param"), P("obs"), P("obs"), P())
    return jax.shard_map(
        per_device,
        mesh=mesh,
        in_specs=placed,
        out_specs=(P("obs", "param"), P("param"), P("obs")),
        check_vma=False,
    )
```

time: 535 us -> 165 us (0.31)
  waiting for transfers between devices: 438 us -> 0 us
  Pallas kernels: 0 us -> 154 us
  blocking collectives: 33.3 us -> 0 us
  matrix products: 22.6 us -> 0 us
  other arithmetic: 18.3 us -> 1.27 us
  between operations: 14.1 us -> 0.64 us
    reduce_scatter x1 -> x0, waiting for transfers between devices: 303 us -> none  [per_device(): lax.psum_scatter(lax.dot_general(gathered, weighted, contract, preferred_...]
    pallas_call x0 -> x1, Pallas kernels: none -> 154 us  [per_device(): pl.pallas_call(functools.partial(kernel, 1.0 / total_rows, 1.0 / math.sqr...]
    all_gather x1 -> x0, waiting for transfers between devices: 130 us -> none  [per_device(): gathered = lax.all_gather(filtered, 'param', axis=1, tiled=True)]
    psum x1 -> x0, blocking collectives: 33.3 us -> none  [per_device(): rhs = lax.psum(partial_rhs, 'obs') / math.sqrt(total_rows)]
    dot_general x2 -> x0, matrix products: 22.6 us -> none  [the longest x1 22.3 us: per_device(): lax.dot_general(gathered, weighted, contract, preferred_element_type=jnp....]
    convert_element_type x4 -> x0, other arithmetic: 14.4 us -> none  [the longest x1 7.62 us: per_device(): filtered = apply_filter(design, tails[0], taps).astype(jnp.bfloat16)]
  transfers between devices with their start and end apart: 4 -> 0, of which waited for: 4 -> 0; matrix products, arithmetic and copies ran while one was open for 1% -> 0% of each run, Pallas kernels for 0% -> 0%
where the time goes in v1:
time: 165 us; the launch traced here: 162 us
  Pallas kernels  154 us (93%)
  local copies, waits for them, and re-layouts  6.29 us (4%)
    pallas_call x1, Pallas kernels, per_device(): pl.pallas_call(functools.partial(kernel, 1.0 / total_rows, 1.0 / math.sqr...  154 us
    unnamed x4, local copies, waits for them, and re-layouts  3.76 us

profile of v1, /device:TPU:34, one launch (start us, length us, event | category | flops | bytes accessed | tf_op | source)
XLA Modules:
  0.0 162.4 jit_solution(13498555656716944148)
XLA Ops:
  0.6 1.3 reshape.18.observed
  1.9 1.3 reshape.19.weight
  3.2 154.2 %normal_equations.1 = (f32[512,1024]{1,0:T(8,128)}, f32[8,128]{1,0:T(8,128)}, f32[1,640]{1,0:T(1,128)}) custom-call(bf16[640,1024]{1,0:T(8,128)(2,1)} %design.1, bf16[1,640]{1,0:T(2,128)(2,1)} %reshape.18.observed, f32[1,640]{1,0:T(1,128)} %reshape.19.weight, f32[7]{0:T(128)} %taps.1), custom_call_target="tpu_custom_call" | custom-call | tf_op jit(solution)/shard_map/normal_equations/pallas_call | solution.py:372
  157.4 1.3 reduce
  158.7 0.0 copy-start
  158.7 3.2 %copy.9 = f32[512,1024]{1,0:T(8,128)} copy(f32[512,1024]{1,0:T(8,128)} %get-tuple-element.12) | data formatting | bytes 4194304
  161.8 0.0 copy-done
  161.8 0.6 copy.10
Async XLA Ops:
  158.7 3.2 %copy-start = (f32[8,128]{1,0:T(8,128)S(1)}, f32[8,128]{1,0:T(8,128)}, u32[]{:S(2)}) copy-start(f32[8,128]{1,0:T(8,128)} %get-tuple-element.7) | copy-start | bytes 12292

commit v2 on v1

v2 whole, which is shorter than its diff:
```python
import functools
import math

import jax
import jax.numpy as jnp
from jax import lax
from jax.experimental import pallas as pl
from jax.experimental.pallas import tpu as pltpu
from jax.sharding import PartitionSpec as P

MESH = pl.DeviceIdType.MESH
BF16, F32 = jnp.bfloat16, jnp.float32
ROWS = 640
COLS = 1024
LAGS = 7
PART = 256
DEPTH = 2 * ROWS


def kernel(
    scale, rhs_scale,
    design, observed, weight, taps,
    normal, rhs, filtered_obs,
    ext, halo, obs_tail, obs_halo, wcol, mine, weighted, rows, cols, part, own, taken, far,
    leaving, landed, rhs_all,
    halo_s, halo_r, rows_s, rows_f, rows_sib, rows_r, cols_s, cols_sib, cols_f, cols_r, x_s, x_r, z_s, z_r, rhs_s, rhs_r,
):
    p, o = lax.axis_index("param"), lax.axis_index("obs")
    y, h = p // 2, p % 2
    x, l, k = o // 4, (o // 2) % 2, o % 2
    near = (y - x + 4) % 4
    settled = l == h

    def param_of(y_, h_):
        return ((y_ + 4) % 4) * 2 + h_

    def obs_of(x_, l_, k_):
        return ((x_ + 4) % 4) * 4 + l_ * 2 + k_

    sibling = (p, obs_of(x, l, 1 - k))
    across = (param_of(y, 1 - h), o)
    beside = (p, obs_of(x, 1 - l, k))
    corner = (param_of(y, 1 - h), obs_of(x, 1 - l, k))
    following = (p, (o + 1) % 16)

    def remote(src, dst, send, recv, device):
        return pltpu.make_async_remote_copy(
            src_ref=src, dst_ref=dst, send_sem=send, recv_sem=recv, device_id=device, device_id_type=MESH
        )

    def halo_copies():
        return (
            remote(design.at[pl.ds(ROWS - 16, 16), :], halo, halo_s.at[0], halo_r.at[0], following),
            remote(obs_tail, obs_halo, halo_s.at[1], halo_r.at[1], following),
        )

    def lanes(rel):
        return pl.ds(ROWS * rel, ROWS)

    def span(e):
        return pl.ds(0, PART) if e is None else pl.ds(pl.multiple_of(e * 128, 128), 128)

    def wide(c):
        return pl.ds(c * 512, 512)

    def rows_out(m, rel, e, up):
        target = (param_of(y + 2 * up - 1, h), obs_of(x, l, (k + rel) % 2))
        dy = 1 + 2 * up
        return remote(
            mine.at[rel, m, span(e)], rows.at[dy, m, span(e), lanes(rel)],
            rows_s.at[up, m, rel, e], rows_r.at[dy, m, rel, e], target,
        )

    def rows_on(m, rel, e):
        target = (param_of(y + 1 - 2 * m, h), o)
        return remote(
            rows.at[3 - 2 * m, m, span(e), lanes(rel)], rows.at[2, m, span(e), lanes(rel)],
            rows_f.at[m, rel, e], rows_r.at[2, m, rel, e], target,
        )

    def rows_at(dy, m, rel, e):
        piece = rows.at[dy, m, span(e), lanes(rel)]
        return remote(piece, piece, rows_f.at[0, 0, 0], rows_r.at[dy, m, rel, e], following)

    def rows_over(m, e):
        return remote(mine.at[1, m, span(e)], rows.at[0, m, span(e), lanes(1)], rows_sib.at[m, e], rows_r.at[0, m, 1, e], sibling)

    def cols_over(n):
        half = pl.ds(0, ROWS)
        return remote(cols.at[0, n, half, :], cols.at[0, n, pl.ds(ROWS, ROWS), :], cols_sib.at[n], cols_r.at[0, n, 1], sibling)

    def cols_across(n):
        half = pl.ds(0, ROWS)
        return remote(cols.at[0, n, half, :], cols.at[1, n, half, :], cols_s.at[n], cols_r.at[1, n, 0], across)

    def cols_on(n):
        half = pl.ds(0, ROWS)
        return remote(cols.at[1, n, half, :], cols.at[1, n, pl.ds(ROWS, ROWS), :], cols_f.at[n], cols_r.at[1, n, 1], sibling)

    def beyond(d):
        return (p, obs_of(x + 1 - 2 * d, l, k))

    def x_far(d, q, e=None):
        return remote(part.at[1, d, q, span(e)], far.at[d, q, span(e)], x_s.at[d, 0, q], x_r.at[d, 0, q], beyond(d))

    def x_raw(d, q, e=None):
        dst = taken.at[d, 1 - d, q, span(e)]
        return remote(part.at[2 * d, 1 - d, q, span(e)], dst, x_s.at[d, 1, q], x_r.at[d, 1, q], beyond(d))

    def x_sum(d, q):
        return remote(part.at[2 * d, d, q], taken.at[d, d, q], x_s.at[d, 2, q], x_r.at[d, 2, q], beyond(d))

    def z_home(m, c):
        return remote(leaving.at[0, m, c], landed.at[0, m, c], z_s.at[0, m, c], z_r.at[0, m, c], beside)

    def z_add(m, c):
        return remote(leaving.at[1, m, c], landed.at[1, m, c], z_s.at[1, m, c], z_r.at[1, m, c], beside)

    def z_on(m, c):
        return remote(leaving.at[1, m, c], landed.at[0, m, c], z_s.at[1, m, c], z_r.at[0, m, c], corner)

    def rhs_to(step):
        peer = (p, (o + step) % 16)
        return remote(rhs_all.at[o], rhs_all.at[o], rhs_s.at[step], rhs_r.at[step], peer)

    barrier = pltpu.get_barrier_semaphore()
    greeted = [(param_of(y + step, h), obs_of(x, l, core)) for step in (1, -1) for core in (k, 1 - k)] + [across, corner]
    greeted += [(p, (o + step) % 16) for step in range(1, 16)]
    for device in greeted:
        pl.semaphore_signal(barrier, inc=1, device_id=device, device_id_type=MESH)

    signal_row = jnp.broadcast_to(observed[...].astype(F32), (8, ROWS))
    weight_row = jnp.broadcast_to(weight[...], (8, ROWS))
    obs_tail[...] = signal_row[:, ROWS - 128 :]
    for r in range(ROWS // 128):
        block = jnp.broadcast_to(weight[:, r * 128 : (r + 1) * 128], (128, 128))
        wcol[pl.ds(r * 128, 128), :] = block.T

    def widen(i, _):
        at = pl.multiple_of(i * 128, 128)
        ext[pl.ds(8, ROWS), pl.ds(at, 128)] = design[:, pl.ds(at, 128)].astype(F32)
        return 0

    lax.fori_loop(0, COLS // 128, widen, 0)
    pl.semaphore_wait(barrier, len(greeted))

    @pl.when(o < 15)
    def _():
        for copy in halo_copies():
            copy.start()

    @pl.when(o > 0)
    def _():
        for copy in halo_copies():
            copy.wait_recv()
        ext[pl.ds(0, 8), :] = halo[...].astype(F32)[8:]

    @pl.when(o == 0)
    def _():
        ext[pl.ds(0, 8), :] = jnp.zeros((8, COLS), F32)
        obs_halo[...] = jnp.zeros((8, 128), F32)

    def first_pieces():
        return [rows_out(m, rel, e, 1 - m) for e in range(2) for m in range(2) for rel in (1, 0)]

    def second_pieces():
        return [rows_out(m, rel, e, m) for e in range(2) for m in range(2) for rel in (1, 0)]

    def passed_on(halves=(0, 1)):
        return [rows_on(m, rel, e) for e in halves for m in range(2) for rel in (1, 0)]

    def arrived(dy, m):
        for rel in (1, 0):
            for e in range(2):
                rows_at(dy, m, rel, e).wait_recv()

    def filter_block(i, _):
        e, m, rel = i // 4, (i // 2) % 2, 1 - i % 2
        core = (k + rel) % 2
        within = pl.multiple_of(m * PART + e * 128, 128)
        at = pl.ds(pl.multiple_of(core * 512 + within, 128), 128)
        for r in range(ROWS // 128):
            first = r * 128
            total = ext[pl.ds(8 + first, 128), at]
            for lag in range(1, LAGS + 1):
                total = total + taps[lag - 1] * ext[pl.ds(8 + first - lag, 128), at]
            rounded = total.astype(BF16).astype(F32)
            cols[0, core, pl.ds(first, 128), pl.ds(within, 128)] = (wcol[pl.ds(first, 128), :] * rounded).astype(BF16)
            turned = rounded.T.astype(BF16)
            mine[rel, m, span(e), pl.ds(first, 128)] = turned

            @pl.when(rel == 0)
            def _():
                rows[0, m, span(e), pl.ds(first, 128)] = turned

        rows_out(m, rel, e, 1 - m).start()

        @pl.when(rel == 1)
        def _():
            rows_over(m, e).start()

        return 0

    lax.fori_loop(0, 8, filter_block, 0)
    for n in range(2):
        cols_over(n).start()
        cols_across(n).start()
    first_far = near == 2

    @pl.when(first_far)
    def _():
        for copy in second_pieces():
            copy.start()

    extended = jnp.concatenate([obs_halo[...], signal_row], axis=1)
    total = signal_row
    for lag in range(1, LAGS + 1):
        total = total + taps[lag - 1] * pltpu.roll(extended, lag, 1)[:, 128:]
    filtered_obs[...] = total[0:1, :]
    weighted[...] = jnp.concatenate([weight_row * total, weight_row * total], axis=0).astype(BF16)
    line = lax.broadcasted_iota(jnp.int32, (8, 128), 0)
    sums = jnp.zeros((8, 128), F32)
    for m in range(2):
        for rel in range(2):
            core = (k + rel) % 2
            dots = lax.dot_general(weighted[...], mine[rel, m], (((1,), (1,)), ((), ())), preferred_element_type=F32)
            for c in range(2):
                sums = jnp.where(line == core * 4 + m * 2 + c, dots[0:8, c * 128 : (c + 1) * 128], sums)
    rhs_all[o] = sums
    for step in range(1, 16):
        rhs_to(step).start()

    def multiply(dy, m, q, e=None):
        role = (near + dy) % 4

        def chunk(c, _):
            at = pl.ds(pl.multiple_of(c * 256, 256), 256)
            value = jnp.dot(rows[dy, m, span(e)], cols[q // 2, q % 2, :, at], preferred_element_type=F32)

            @pl.when(role == 0)
            def _():
                own[m, q, span(e), at] = value

            @pl.when(role != 0)
            def _():
                part[role - 1, m, q, span(e), at] = value.astype(BF16)

            return 0

        lax.fori_loop(0, 2, chunk, 0)

        @pl.when(role == 2)
        def _():
            x_far(m, q, e).start()

        @pl.when(jnp.logical_or(jnp.logical_and(role == 1, m == 1), jnp.logical_and(role == 3, m == 0)))
        def _():
            x_raw(role // 2, q, e).start()

    def add_far(d, q, valid=True):
        @pl.when(valid)
        def _():
            x_far(d, q).wait_recv()
            part[2 * d, d, q] = (part[2 * d, d, q].astype(F32) + far[d, q].astype(F32)).astype(BF16)
            x_sum(d, q).start()

    def by_near(*values):
        chosen = values[3]
        for place in (2, 1, 0):
            chosen = jnp.where(near == place, values[place], chosen)
        return chosen

    for m in range(2):
        for e in range(2):
            rows_over(m, e).wait_recv()
        cols_over(m).wait_recv()
    for q in range(2):
        for m in (1, 0):
            multiply(0, m, q)

    for e in range(2):
        for m in range(2):
            for rel in (1, 0):
                rows_at(3 - 2 * m, m, rel, e).wait_recv()
        for copy in passed_on((e,)):
            copy.start()
        if e == 1:

            @pl.when(jnp.logical_not(first_far))
            def _():
                for copy in second_pieces():
                    copy.start()

        for q in range(2):
            multiply(3, 0, q, e)
            multiply(1, 1, q, e)
        add_far(by_near(0, 0, 0, 1), e, (near % 2) == 1)
    cols_across(0).wait_recv()
    cols_on(0).start()
    cols_on(0).wait_recv()
    for m in (1, 0):
        multiply(0, m, 2)
    multiply(3, 0, 2)
    multiply(1, 1, 2)
    for q in range(2):
        for d in range(2):
            add_far(d, q, near == 2)
    add_far(by_near(0, 0, 0, 1), 2, (near % 2) == 1)

    third = (by_near(2, 1, 2, 3), by_near(0, 0, 0, 1))
    fourth = (2, by_near(1, 0, 1, 1))
    fifth = (by_near(1, 2, 1, 2), by_near(0, 1, 0, 0))
    sixth = (by_near(3, 3, 3, 1), by_near(1, 1, 1, 0))
    arrived(*third)
    multiply(*third, 0)
    arrived(*fourth)
    multiply(*fourth, 0)
    for q in (1, 2):
        multiply(*third, q)
        multiply(*fourth, q)
    cols_across(1).wait_recv()
    cols_on(1).start()
    cols_on(1).wait_recv()
    multiply(*third, 3)
    multiply(*fourth, 3)
    for m in (1, 0):
        multiply(0, m, 3)
    multiply(3, 0, 3)
    multiply(1, 1, 3)

    add_far(by_near(0, 0, 0, 1), by_near(0, 3, 2, 3), near != 0)
    add_far(1, 2, near == 2)

    for piece in (fifth, sixth):
        arrived(*piece)
    for q in (0, 2, 3, 1):
        for piece in (fifth, sixth):
            multiply(*piece, q)
    for q in (0, 2, 3, 1):
        add_far(by_near(0, 1, 0, 0), q, jnp.logical_or(near != 2, q == 3))
        add_far(1, q, jnp.logical_or(near == 0, jnp.logical_and(near == 2, q == 3)))

    for step in range(1, 16):
        rhs_to(step).wait_recv()
    total = rhs_all[0]
    for step in range(1, 16):
        total = total + rhs_all[step]
    rhs[...] = total * rhs_scale

    def summed(m, q):
        x_sum(m, q).wait_recv()
        x_raw(1 - m, q).wait_recv()
        return own[m, q] + taken[0, m, q].astype(F32) + taken[1, m, q].astype(F32)

    def keep_near(c):
        for m in range(2):
            total = summed(m, c)

            @pl.when(settled)
            def _():
                own[m, c] = total

            @pl.when(jnp.logical_not(settled))
            def _():
                leaving[0, m, c] = total.astype(BF16)
                z_home(m, c).start()

    def pass_over(c):
        for m in range(2):
            total = summed(m, 2 + c)

            @pl.when(settled)
            def _():
                leaving[1, m, c] = total.astype(BF16)
                z_add(m, c).start()

            @pl.when(jnp.logical_not(settled))
            def _():
                own[m, 2 + c] = total

    def pass_on(c):
        @pl.when(jnp.logical_not(settled))
        def _():
            for m in range(2):
                z_add(m, c).wait_recv()
                leaving[1, m, c] = (own[m, 2 + c] + landed[1, m, c].astype(F32)).astype(BF16)
                z_on(m, c).start()

    keep_near(0)
    pass_over(0)
    pass_over(1)
    pass_on(0)
    keep_near(1)
    pass_on(1)

    for c in range(2):
        for m in range(2):
            z_home(m, c).wait_recv()
            at = pl.ds(m * PART, PART)

            @pl.when(settled)
            def _():
                normal[at, wide(c)] = (own[m, c] + landed[0, m, c].astype(F32)) * scale

            @pl.when(jnp.logical_not(settled))
            def _():
                normal[at, wide(c)] = landed[0, m, c].astype(F32) * scale

    @pl.when(o < 15)
    def _():
        for copy in halo_copies():
            copy.wait_send()

    for m in range(2):
        for e in range(2):
            rows_over(m, e).wait_send()
        cols_over(m).wait_send()
        cols_across(m).wait_send()
        cols_on(m).wait_send()
        for c in range(2):
            z_add(m, c).wait_send()

        @pl.when(jnp.logical_not(settled))
        def _():
            for c in range(2):
                z_home(m, c).wait_send()

        for q in range(4):
            x_far(m, q).wait_send()
            x_raw(m, q).wait_send()
            x_sum(m, q).wait_send()
    for copy in first_pieces() + passed_on() + second_pieces():
        copy.wait_send()
    for step in range(1, 16):
        rhs_to(step).wait_send()


def per_device(design, observed, row_weight, taps):
    total_rows = ROWS * lax.axis_size("obs")
    dma = pltpu.SemaphoreType.DMA
    vmem = pl.BlockSpec(memory_space=pltpu.VMEM)
    normal, rhs, filtered_obs = pl.pallas_call(
        functools.partial(kernel, 1.0 / total_rows, 1.0 / math.sqrt(total_rows)),
        out_shape=(
            jax.ShapeDtypeStruct((512, COLS), F32),
            jax.ShapeDtypeStruct((8, 128), F32),
            jax.ShapeDtypeStruct((1, ROWS), F32),
        ),
        in_specs=[vmem, vmem, vmem, pl.BlockSpec(memory_space=pltpu.SMEM)],
        out_specs=(vmem, vmem, vmem),
        scratch_shapes=[
            pltpu.VMEM((ROWS + 8, COLS), F32),
            pltpu.VMEM((16, COLS), BF16),
            pltpu.VMEM((8, 128), F32),
            pltpu.VMEM((8, 128), F32),
            pltpu.VMEM((ROWS, 128), F32),
            pltpu.VMEM((2, 2, PART, ROWS), BF16),
            pltpu.VMEM((16, ROWS), BF16),
            pltpu.VMEM((4, 2, PART, DEPTH), BF16),
            pltpu.VMEM((2, 2, DEPTH, 512), BF16),
            pltpu.VMEM((3, 2, 4, PART, 512), BF16),
            pltpu.VMEM((2, 4, PART, 512), F32),
            pltpu.VMEM((2, 2, 4, PART, 512), BF16),
            pltpu.VMEM((2, 4, PART, 512), BF16),
            pltpu.VMEM((2, 2, 2, PART, 512), BF16),
            pltpu.VMEM((2, 2, 2, PART, 512), BF16),
            pltpu.VMEM((16, 8, 128), F32),
            dma((2,)), dma((2,)),
            dma((2, 2, 2, 2)), dma((2, 2, 2)), dma((2, 2)), dma((4, 2, 2, 2)),
            dma((2,)), dma((2,)), dma((2,)), dma((2, 2, 2)),
            dma((2, 3, 4)), dma((2, 3, 4)),
            dma((2, 2, 2)), dma((2, 2, 2)),
            dma((16,)), dma((16,)),
        ],
        compiler_params=pltpu.CompilerParams(collective_id=0, has_side_effects=True, vmem_limit_bytes=60 << 20),
        name="normal_equations",
    )(design, observed.reshape(1, ROWS), row_weight.reshape(1, ROWS), taps)
    return normal, rhs.reshape(COLS), filtered_obs.reshape(ROWS)


def solution(mesh):
    placed = (P("obs", "param"), P("obs"), P("obs"), P())
    return jax.shard_map(
        per_device,
        mesh=mesh,
        in_specs=placed,
        out_specs=(P("obs", "param"), P("param"), P("obs")),
        check_vma=False,
    )
```

time: 165 us -> 128 us (0.78)
  Pallas kernels: 154 us -> 118 us
    pallas_call x1, Pallas kernels: 154 us -> 118 us  [per_device(): pl.pallas_call(functools.partial(kernel, 1.0 / total_rows, 1.0 / math.sqr...]
where the time goes in v2:
time: 128 us; the launch traced here: 126 us
  Pallas kernels  118 us (92%)
  local copies, waits for them, and re-layouts  6.29 us (5%)
    pallas_call x1, Pallas kernels, per_device(): pl.pallas_call(functools.partial(kernel, 1.0 / total_rows, 1.0 / math.sqr...  118 us
    unnamed x4, local copies, waits for them, and re-layouts  3.76 us

profile of v2, /device:TPU:34, one launch (start us, length us, event | category | flops | bytes accessed | tf_op | source)
XLA Modules:
  0.0 126.3 jit_solution(17645298720949524343)
XLA Ops:
  0.6 1.3 %reshape.18.observed = bf16[1,640]{1,0:T(2,128)(2,1)} reshape(bf16[640]{0:T(1024)(128)(2,1)} %param.5) | data formatting | bytes 2560 | tf_op jit(solution)/shard_map/reshape | solution.py:477
  1.9 1.3 %reshape.19.weight = f32[1,640]{1,0:T(1,128)} reshape(f32[640]{0:T(1024)} %param.6) | data formatting | bytes 5120 | tf_op jit(solution)/shard_map/reshape | solution.py:477
  3.2 118.1 %normal_equations.1 = (f32[512,1024]{1,0:T(8,128)}, f32[8,128]{1,0:T(8,128)}, f32[1,640]{1,0:T(1,128)}) custom-call(bf16[640,1024]{1,0:T(8,128)(2,1)} %design.1, bf16[1,640]{1,0:T(2,128)(2,1)} %reshape.18.observed, f32[1,640]{1,0:T(1,128)} %reshape.19.weight, f32[7]{0:T(128)} %taps.1), custom_call_target="tpu_custom_call" | custom-call | tf_op jit(solution)/shard_map/normal_equations/pallas_call | solution.py:442
  121.3 1.3 %reduce = f32[640]{0:T(1024)} reduce(f32[1,640]{1,0:T(1,128)} %get-tuple-element.8, f32[]{:T(128)} %constant), dimensions={0}, to_apply=%get-tuple-element.8.reduce_sub_computation | reduce | bytes 5124 | tf_op jit(solution)/shard_map/normal_equations/pallas_call | solution.py:442
  122.5 0.0 copy-start
  122.5 3.2 %copy.9 = f32[512,1024]{1,0:T(8,128)} copy(f32[512,1024]{1,0:T(8,128)} %get-tuple-element.12) | data formatting | bytes 4194304
  125.7 0.0 copy-done
  125.7 0.6 copy.10
Async XLA Ops:
  122.5 3.2 %copy-start = (f32[8,128]{1,0:T(8,128)S(1)}, f32[8,128]{1,0:T(8,128)}, u32[]{:S(2)}) copy-start(f32[8,128]{1,0:T(8,128)} %get-tuple-element.7) | copy-start | bytes 12292

commit v3 on v2

v3 whole, which is shorter than its diff:
```python
import functools
import math

import jax
import jax.numpy as jnp
from jax import lax
from jax.experimental import pallas as pl
from jax.experimental.pallas import tpu as pltpu
from jax.sharding import PartitionSpec as P

MESH = pl.DeviceIdType.MESH
BF16, F32 = jnp.bfloat16, jnp.float32
ROWS = 640
COLS = 1024
LAGS = 7
PART = 256
DEPTH = 2 * ROWS


def kernel(
    scale, rhs_scale,
    design_hbm, observed, weight, taps,
    normal, rhs, filtered_obs,
    design, ext, halo, obs_tail, obs_halo, wcol, mine, weighted, rows, cols, part, own, taken, far,
    leaving, landed, passing, rhs_all,
    design_s, halo_s, halo_r, rows_s, rows_f, rows_sib, rows_r, cols_s, cols_sib, cols_f, cols_r, x_s, x_r, z_s, z_r, z_fs, z_fr, rhs_s, rhs_r,
):
    p, o = lax.axis_index("param"), lax.axis_index("obs")
    y, h = p // 2, p % 2
    x, l, k = o // 4, (o // 2) % 2, o % 2
    near = (y - x + 4) % 4
    settled = l == h

    def param_of(y_, h_):
        return ((y_ + 4) % 4) * 2 + h_

    def obs_of(x_, l_, k_):
        return ((x_ + 4) % 4) * 4 + l_ * 2 + k_

    sibling = (p, obs_of(x, l, 1 - k))
    across = (param_of(y, 1 - h), o)
    beside = (p, obs_of(x, 1 - l, k))
    corner = (param_of(y, 1 - h), obs_of(x, 1 - l, k))
    following = (p, (o + 1) % 16)

    def remote(src, dst, send, recv, device):
        return pltpu.make_async_remote_copy(
            src_ref=src, dst_ref=dst, send_sem=send, recv_sem=recv, device_id=device, device_id_type=MESH
        )

    def halo_copies():
        return (
            remote(design.at[pl.ds(ROWS - 16, 16), :], halo, halo_s.at[0], halo_r.at[0], following),
            remote(obs_tail, obs_halo, halo_s.at[1], halo_r.at[1], following),
        )

    def lanes(rel):
        return pl.ds(ROWS * rel, ROWS)

    def span(e):
        return pl.ds(0, PART) if e is None else pl.ds(pl.multiple_of(e * 128, 128), 128)

    def wide(c):
        return pl.ds(c * 512, 512)

    def rows_out(m, rel, e, up):
        target = (param_of(y + 2 * up - 1, h), obs_of(x, l, (k + rel) % 2))
        dy = 1 + 2 * up
        return remote(
            mine.at[rel, m, span(e)], rows.at[dy, m, span(e), lanes(rel)],
            rows_s.at[up, m, rel, e], rows_r.at[dy, m, rel, e], target,
        )

    def rows_on(m, rel, e):
        target = (param_of(y + 1 - 2 * m, h), o)
        return remote(
            rows.at[3 - 2 * m, m, span(e), lanes(rel)], rows.at[2, m, span(e), lanes(rel)],
            rows_f.at[m, rel, e], rows_r.at[2, m, rel, e], target,
        )

    def rows_at(dy, m, rel, e):
        piece = rows.at[dy, m, span(e), lanes(rel)]
        return remote(piece, piece, rows_f.at[0, 0, 0], rows_r.at[dy, m, rel, e], following)

    def rows_over(m, e):
        return remote(mine.at[1, m, span(e)], rows.at[0, m, span(e), lanes(1)], rows_sib.at[m, e], rows_r.at[0, m, 1, e], sibling)

    def cols_over(n):
        half = pl.ds(0, ROWS)
        return remote(cols.at[0, n, half, :], cols.at[0, n, pl.ds(ROWS, ROWS), :], cols_sib.at[n], cols_r.at[0, n, 1], sibling)

    def cols_across(n):
        half = pl.ds(0, ROWS)
        return remote(cols.at[0, n, half, :], cols.at[1, n, half, :], cols_s.at[n], cols_r.at[1, n, 0], across)

    def cols_on(n):
        half = pl.ds(0, ROWS)
        return remote(cols.at[1, n, half, :], cols.at[1, n, pl.ds(ROWS, ROWS), :], cols_f.at[n], cols_r.at[1, n, 1], sibling)

    def beyond(d):
        return (p, obs_of(x + 1 - 2 * d, l, k))

    def x_far(d, q, e=None):
        return remote(part.at[1, d, q, span(e)], far.at[d, q, span(e)], x_s.at[d, 0, q], x_r.at[d, 0, q], beyond(d))

    def x_raw(d, q, e=None):
        dst = taken.at[d, 1 - d, q, span(e)]
        return remote(part.at[2 * d, 1 - d, q, span(e)], dst, x_s.at[d, 1, q], x_r.at[d, 1, q], beyond(d))

    def x_sum(d, q, e=None):
        kind = 2 if e is None else 2 + e
        return remote(
            part.at[2 * d, d, q, span(e)], taken.at[d, d, q, span(e)], x_s.at[d, kind, q], x_r.at[d, kind, q], beyond(d)
        )

    def z_home(m, c, e=None):
        sem = c if e is None else c + e
        return remote(leaving.at[0, m, c, span(e)], landed.at[0, m, c, span(e)], z_s.at[0, m, sem], z_r.at[0, m, sem], beside)

    def z_add(c):
        return remote(leaving.at[1, 0, c], landed.at[1, 0, c], z_s.at[1, 0, c], z_r.at[1, 0, c], beside)

    def z_on(m, c):
        return remote(leaving.at[1, m, c], landed.at[0, m, c], z_s.at[1, m, c], z_r.at[0, m, c], corner)

    def z_via(c):
        return remote(leaving.at[1, 1, c], passing.at[c], z_s.at[1, 1, c], z_r.at[1, 1, c], corner)

    def z_fwd(c):
        return remote(passing.at[c], landed.at[1, 1, c], z_fs.at[c], z_fr.at[c], beside)

    def rhs_to(step):
        peer = (p, (o + step) % 16)
        return remote(rhs_all.at[o], rhs_all.at[o], rhs_s.at[step], rhs_r.at[step], peer)

    incoming = pltpu.make_async_copy(design_hbm, design, design_s)
    incoming.start()

    barrier = pltpu.get_barrier_semaphore()
    greeted = [(param_of(y + step, h), obs_of(x, l, core)) for step in (1, -1) for core in (k, 1 - k)] + [across, corner]
    greeted += [(p, (o + step) % 16) for step in range(1, 16)]
    for device in greeted:
        pl.semaphore_signal(barrier, inc=1, device_id=device, device_id_type=MESH)

    signal_row = jnp.broadcast_to(observed[...].astype(F32).reshape(1, ROWS), (8, ROWS))
    weight_row = jnp.broadcast_to(weight[...].reshape(1, ROWS), (8, ROWS))
    obs_tail[...] = signal_row[:, ROWS - 128 :]
    for r in range(ROWS // 128):
        block = jnp.broadcast_to(weight_row[0:1, r * 128 : (r + 1) * 128], (128, 128))
        wcol[pl.ds(r * 128, 128), :] = block.T

    def widen(i, _):
        at = pl.multiple_of(i * 128, 128)
        ext[pl.ds(8, ROWS), pl.ds(at, 128)] = design[:, pl.ds(at, 128)].astype(F32)
        return 0

    incoming.wait()
    lax.fori_loop(0, COLS // 128, widen, 0)

    def filter_rows(i, r):
        e, m, rel = i // 4, (i // 2) % 2, 1 - i % 2
        core = (k + rel) % 2
        at = pl.ds(pl.multiple_of(core * 512 + m * PART + e * 128, 128), 128)
        quarter = pl.ds(pl.multiple_of((core * 2 + m) * 128, 128), 128)
        first = r * 128
        total = ext[pl.ds(8 + first, 128), at]
        for lag in range(1, LAGS + 1):
            total = total + taps[lag - 1] * ext[pl.ds(8 + first - lag, 128), at]
        rounded = total.astype(BF16).astype(F32)
        cols[0, e, pl.ds(first, 128), quarter] = (wcol[pl.ds(first, 128), :] * rounded).astype(BF16)
        turned = rounded.T.astype(BF16)
        mine[rel, m, span(e), pl.ds(first, 128)] = turned

        @pl.when(rel == 0)
        def _():
            rows[0, m, span(e), pl.ds(first, 128)] = turned

    def filter_later_rows(i, _):
        for r in range(1, ROWS // 128):
            filter_rows(i, r)
        return 0

    lax.fori_loop(0, 4, filter_later_rows, 0)
    pl.semaphore_wait(barrier, len(greeted))

    @pl.when(o < 15)
    def _():
        for copy in halo_copies():
            copy.start()

    lax.fori_loop(4, 8, filter_later_rows, 0)

    @pl.when(o > 0)
    def _():
        for copy in halo_copies():
            copy.wait_recv()
        ext[pl.ds(0, 8), :] = halo[...].astype(F32)[8:]

    @pl.when(o == 0)
    def _():
        ext[pl.ds(0, 8), :] = jnp.zeros((8, COLS), F32)
        obs_halo[...] = jnp.zeros((8, 128), F32)

    def first_pieces():
        return [rows_out(m, rel, e, 1 - m) for e in range(2) for m in range(2) for rel in (1, 0)]

    def second_pieces():
        return [rows_out(m, rel, e, m) for e in range(2) for m in range(2) for rel in (1, 0)]

    def passed_on(halves=(0, 1)):
        return [rows_on(m, rel, e) for e in halves for m in range(2) for rel in (1, 0)]

    def arrived(dy, m):
        for rel in (1, 0):
            for e in range(2):
                rows_at(dy, m, rel, e).wait_recv()

    def filter_block(i, _):
        e, m, rel = i // 4, (i // 2) % 2, 1 - i % 2
        filter_rows(i, 0)
        rows_out(m, rel, e, 1 - m).start()

        @pl.when(rel == 1)
        def _():
            rows_over(m, e).start()

        @pl.when(i == 3)
        def _():
            cols_over(0).start()
            cols_across(0).start()

        return 0

    lax.fori_loop(0, 8, filter_block, 0)
    cols_over(1).start()
    cols_across(1).start()
    first_far = near == 2

    @pl.when(first_far)
    def _():
        for copy in second_pieces():
            copy.start()

    def multiply(dy, m, q, e=None):
        role = (near + dy) % 4

        def chunk(c, _):
            at = pl.ds(pl.multiple_of(c * 256, 256), 256)
            value = jnp.dot(rows[dy, m, span(e)], cols[q // 2, q % 2, :, at], preferred_element_type=F32)

            @pl.when(role == 0)
            def _():
                own[m, q, span(e), at] = value

            @pl.when(role != 0)
            def _():
                part[role - 1, m, q, span(e), at] = value.astype(BF16)

            return 0

        lax.fori_loop(0, 2, chunk, 0)

        @pl.when(role == 2)
        def _():
            x_far(m, q, e).start()

        @pl.when(jnp.logical_or(jnp.logical_and(role == 1, m == 1), jnp.logical_and(role == 3, m == 0)))
        def _():
            x_raw(role // 2, q, e).start()

    def add_far(d, q, valid=True):
        @pl.when(valid)
        def _():
            x_far(d, q).wait_recv()
            for e in halves_of(q):
                both = part[2 * d, d, q, span(e)].astype(F32) + far[d, q, span(e)].astype(F32)
                part[2 * d, d, q, span(e)] = both.astype(BF16)
                x_sum(d, q, e).start()

    def halves_of(q):
        return (0, 1) if isinstance(q, int) and q == 1 else (None,)

    def by_near(*values):
        chosen = values[3]
        for place in (2, 1, 0):
            chosen = jnp.where(near == place, values[place], chosen)
        return chosen

    for m in range(2):
        for e in range(2):
            rows_over(m, e).wait_recv()
        cols_over(m).wait_recv()
    for q in range(2):
        for m in (1, 0):
            multiply(0, m, q)

    for e in range(2):
        for m in range(2):
            for rel in (1, 0):
                rows_at(3 - 2 * m, m, rel, e).wait_recv()
        for copy in passed_on((e,)):
            copy.start()
        if e == 1:

            @pl.when(jnp.logical_not(first_far))
            def _():
                for copy in second_pieces():
                    copy.start()

        for q in range(2):
            multiply(3, 0, q, e)
            multiply(1, 1, q, e)
        add_far(by_near(0, 0, 0, 1), e, (near % 2) == 1)
    cols_across(0).wait_recv()
    cols_on(0).start()
    cols_on(0).wait_recv()
    multiply(by_near(3, 0, 0, 0), by_near(0, 1, 1, 1), 2)
    multiply(by_near(1, 0, 0, 0), by_near(1, 0, 0, 0), 2)
    multiply(by_near(0, 3, 3, 3), by_near(1, 0, 0, 0), 2)
    multiply(by_near(0, 1, 1, 1), by_near(0, 1, 1, 1), 2)
    for q in range(2):
        for d in range(2):
            add_far(d, q, near == 2)

    extended = jnp.concatenate([obs_halo[...], signal_row], axis=1)
    total = signal_row
    for lag in range(1, LAGS + 1):
        total = total + taps[lag - 1] * pltpu.roll(extended, lag, 1)[:, 128:]
    filtered_obs[...] = total[0:1, :].reshape(ROWS)
    weighted[...] = jnp.concatenate([weight_row * total, weight_row * total], axis=0).astype(BF16)
    line = lax.broadcasted_iota(jnp.int32, (8, 128), 0)
    sums = jnp.zeros((8, 128), F32)
    for m in range(2):
        for rel in range(2):
            core = (k + rel) % 2
            dots = lax.dot_general(weighted[...], mine[rel, m], (((1,), (1,)), ((), ())), preferred_element_type=F32)
            for c in range(2):
                sums = jnp.where(line == core * 4 + m * 2 + c, dots[0:8, c * 128 : (c + 1) * 128], sums)
    rhs_all[o] = sums
    for step in range(1, 16):
        rhs_to(step).start()

    third = (by_near(2, 1, 2, 3), by_near(0, 0, 0, 1))
    fourth = (2, by_near(1, 0, 1, 1))
    fifth = (by_near(1, 2, 1, 2), by_near(0, 1, 0, 0))
    sixth = (by_near(3, 3, 3, 1), by_near(1, 1, 1, 0))
    arrived(*third)
    multiply(*third, 0)
    arrived(*fourth)
    multiply(*fourth, 0)
    multiply(*third, 2)
    multiply(*fourth, 2)
    cols_across(1).wait_recv()
    cols_on(1).start()
    cols_on(1).wait_recv()

    def last_sums(q, valid=True):
        add_far(by_near(0, 1, 0, 0), q, valid)
        add_far(1, q, jnp.logical_and(valid, (near % 2) == 0))

    multiply(by_near(2, 1, 0, 3), by_near(0, 0, 1, 1), 3)
    multiply(by_near(2, 1, 0, 3), by_near(1, 1, 0, 0), 3)
    add_far(by_near(0, 0, 0, 1), 2, near != 0)
    add_far(1, 2, near == 2)
    multiply(by_near(3, 0, 3, 0), by_near(0, 0, 0, 1), 3)
    multiply(by_near(1, 0, 1, 0), by_near(1, 1, 1, 0), 3)

    @pl.when(near != 0)
    def _():
        multiply(*third, 1)
        multiply(*fourth, 1)

    multiply(by_near(0, 2, 2, 2), by_near(0, 0, 0, 1), 3)
    multiply(by_near(0, 3, 2, 1), by_near(1, 0, 1, 1), 3)
    for piece in (fifth, sixth):
        arrived(*piece)
    for q in (0, 2):
        for piece in (fifth, sixth):
            multiply(*piece, q)
        last_sums(q, near != 2)
    add_far(by_near(0, 0, 0, 1), 3, (near % 2) == 1)
    for piece in (fifth, sixth):
        multiply(*piece, 3)

    @pl.when(near == 0)
    def _():
        multiply(*third, 1)
        multiply(*fourth, 1)

    last_sums(3)
    for piece in (fifth, sixth):
        multiply(*piece, 1)
    last_sums(1, near == 0)

    for step in range(1, 16):
        rhs_to(step).wait_recv()
    total = rhs_all[0]
    for step in range(1, 16):
        total = total + rhs_all[step]
    rhs[...] = (total * rhs_scale).reshape(COLS)

    def summed(m, q, e=None):
        x_sum(m, q, e).wait_recv()
        if not e:
            x_raw(1 - m, q).wait_recv()
        return own[m, q, span(e)] + taken[0, m, q, span(e)].astype(F32) + taken[1, m, q, span(e)].astype(F32)

    def keep_near(c):
        for e in halves_of(c):
            for m in range(2):
                total = summed(m, c, e)

                @pl.when(settled)
                def _():
                    own[m, c, span(e)] = total

                @pl.when(jnp.logical_not(settled))
                def _():
                    leaving[0, m, c, span(e)] = total.astype(BF16)
                    z_home(m, c, e).start()

    def pass_over(c):
        for m in (1, 0):
            total = summed(m, 2 + c)

            @pl.when(settled)
            def _():
                leaving[1, m, c] = total.astype(BF16)
                (z_add(c) if m == 0 else z_via(c)).start()

            @pl.when(jnp.logical_not(settled))
            def _():
                if m == 0:
                    own[m, 2 + c] = total
                else:
                    leaving[1, m, c] = total.astype(BF16)
                    z_on(m, c).start()

    def pass_on(c):
        @pl.when(settled)
        def _():
            z_via(c).wait_recv()
            z_fwd(c).start()

        @pl.when(jnp.logical_not(settled))
        def _():
            z_add(c).wait_recv()
            leaving[1, 0, c] = (own[0, 2 + c] + landed[1, 0, c].astype(F32)).astype(BF16)
            z_on(0, c).start()

    keep_near(0)
    pass_over(0)
    last_sums(1, (near % 2) == 1)
    pass_over(1)
    pass_on(0)
    keep_near(1)
    pass_on(1)

    def place(m, c, total):
        for b in range(4):
            to = pl.ds(b // 2 * 512 + b % 2 * 256 + c * 128, 128)
            normal[pl.ds(m * PART, PART), to] = total[:, b * 128 : b * 128 + 128] * scale

    for c in range(2):
        for m in range(2):

            @pl.when(settled)
            def _():
                for e in halves_of(c):
                    z_home(m, c, e).wait_recv()
                place(m, c, own[m, c] + landed[0, m, c].astype(F32))

            @pl.when(jnp.logical_not(settled))
            def _():
                z_on(m, c).wait_recv()
                total = landed[0, m, c].astype(F32)
                if m == 1:
                    z_fwd(c).wait_recv()
                    total = total + landed[1, 1, c].astype(F32)
                place(m, c, total)

    @pl.when(o < 15)
    def _():
        for copy in halo_copies():
            copy.wait_send()

    for m in range(2):
        for e in range(2):
            rows_over(m, e).wait_send()
        cols_over(m).wait_send()
        cols_across(m).wait_send()
        cols_on(m).wait_send()
        for c in range(2):
            z_on(m, c).wait_send()

            @pl.when(jnp.logical_not(settled))
            def _():
                for e in halves_of(c):
                    z_home(m, c, e).wait_send()

        @pl.when(settled)
        def _():
            z_fwd(m).wait_send()

        for q in range(4):
            x_far(m, q).wait_send()
            x_raw(m, q).wait_send()
            for e in halves_of(q):
                x_sum(m, q, e).wait_send()
    for copy in first_pieces() + passed_on() + second_pieces():
        copy.wait_send()
    for step in range(1, 16):
        rhs_to(step).wait_send()


def per_device(design, observed, row_weight, taps):
    total_rows = ROWS * lax.axis_size("obs")
    dma = pltpu.SemaphoreType.DMA
    vmem = pl.BlockSpec(memory_space=pltpu.VMEM)
    normal, rhs, filtered_obs = pl.pallas_call(
        functools.partial(kernel, 1.0 / total_rows, 1.0 / math.sqrt(total_rows)),
        out_shape=(
            jax.ShapeDtypeStruct((512, COLS), F32),
            jax.ShapeDtypeStruct((COLS,), F32),
            jax.ShapeDtypeStruct((ROWS,), F32),
        ),
        in_specs=[pl.BlockSpec(memory_space=pl.ANY), vmem, vmem, pl.BlockSpec(memory_space=pltpu.SMEM)],
        out_specs=(vmem, vmem, vmem),
        scratch_shapes=[
            pltpu.VMEM((ROWS, COLS), BF16),
            pltpu.VMEM((ROWS + 8, COLS), F32),
            pltpu.VMEM((16, COLS), BF16),
            pltpu.VMEM((8, 128), F32),
            pltpu.VMEM((8, 128), F32),
            pltpu.VMEM((ROWS, 128), F32),
            pltpu.VMEM((2, 2, PART, ROWS), BF16),
            pltpu.VMEM((16, ROWS), BF16),
            pltpu.VMEM((4, 2, PART, DEPTH), BF16),
            pltpu.VMEM((2, 2, DEPTH, 512), BF16),
            pltpu.VMEM((3, 2, 4, PART, 512), BF16),
            pltpu.VMEM((2, 4, PART, 512), F32),
            pltpu.VMEM((2, 2, 4, PART, 512), BF16),
            pltpu.VMEM((2, 4, PART, 512), BF16),
            pltpu.VMEM((2, 2, 2, PART, 512), BF16),
            pltpu.VMEM((2, 2, 2, PART, 512), BF16),
            pltpu.VMEM((2, PART, 512), BF16),
            pltpu.VMEM((16, 8, 128), F32),
            dma, dma((2,)), dma((2,)),
            dma((2, 2, 2, 2)), dma((2, 2, 2)), dma((2, 2)), dma((4, 2, 2, 2)),
            dma((2,)), dma((2,)), dma((2,)), dma((2, 2, 2)),
            dma((2, 4, 4)), dma((2, 4, 4)),
            dma((2, 2, 3)), dma((2, 2, 3)), dma((2,)), dma((2,)),
            dma((16,)), dma((16,)),
        ],
        compiler_params=pltpu.CompilerParams(collective_id=0, has_side_effects=True, vmem_limit_bytes=60 << 20),
        name="normal_equations",
    )(design, observed, row_weight, taps)
    return normal, rhs, filtered_obs


def solution(mesh):
    placed = (P("obs", "param"), P("obs"), P("obs"), P())
    return jax.shard_map(
        per_device,
        mesh=mesh,
        in_specs=placed,
        out_specs=(P("obs", "param"), P("param"), P("obs")),
        check_vma=False,
    )
```

time: 128 us -> 115 us (0.90)
  the two profiles are of different devices: /device:TPU:34 before, /device:TPU:80 now
where the time goes in v3:
time: 115 us
  Pallas kernels  110 us (96%)
  local copies, waits for them, and re-layouts  4.36 us (4%)
    pallas_call x1, Pallas kernels, per_device(): pl.pallas_call(functools.partial(kernel, 1.0 / total_rows, 1.0 / math.sqr...  110 us
    unnamed x7, local copies, waits for them, and re-layouts  4.36 us

profile of v3, /device:TPU:80, one launch (start us, length us, event | category | flops | bytes accessed | tf_op | source)
XLA Modules:
  0.0 114.7 jit_solution(1667757263871476605)
XLA Ops:
  0.6 109.7 %normal_equations.1 = (f32[512,1024]{1,0:T(8,128)}, f32[1024]{0:T(1024)}, f32[640]{0:T(1024)}) custom-call(bf16[640,1024]{1,0:T(8,128)(2,1)} %design_hbm.1, bf16[640]{0:T(1024)(128)(2,1)} %observed.1, f32[640]{0:T(1024)} %weight.1, f32[7]{0:T(128)} %taps.1), custom_call_target="tpu_custom_call" | custom-call | tf_op jit(solution)/shard_map/normal_equations/pallas_call | solution.py:520
  110.3 0.0 copy-start.1
  110.3 0.0 copy-start
  110.3 3.2 %copy.10 = f32[512,1024]{1,0:T(8,128)} copy(f32[512,1024]{1,0:T(8,128)} %get-tuple-element.6) | data formatting | bytes 4194304
  113.5 0.0 copy-done.1
  113.5 0.6 copy.11
  114.1 0.0 copy-done
  114.1 0.6 copy.12
Async XLA Ops:
  110.3 3.2 %copy-start.1 = (f32[1024]{0:T(1024)S(1)}, f32[1024]{0:T(1024)}, u32[]{:S(2)}) copy-start(f32[1024]{0:T(1024)} %get-tuple-element.7) | copy-start | bytes 12292
  110.3 3.8 %copy-start = (f32[640]{0:T(1024)S(1)}, f32[640]{0:T(1024)}, u32[]{:S(2)}) copy-start(f32[640]{0:T(1024)} %get-tuple-element.8) | copy-start | bytes 7684

commit v4 on v3

--- a/solution.py
+++ b/solution.py
@@ -63,11 +63,12 @@
     def wide(c):
         return pl.ds(c * 512, 512)
 
-    def rows_out(m, rel, e, up):
+    def rows_out(m, rel, e, up, begin=0, end=ROWS):
         target = (param_of(y + 2 * up - 1, h), obs_of(x, l, (k + rel) % 2))
         dy = 1 + 2 * up
+        to = pl.ds(pl.multiple_of(ROWS * rel + begin, 128), end - begin)
         return remote(
-            mine.at[rel, m, span(e)], rows.at[dy, m, span(e), lanes(rel)],
+            mine.at[rel, m, span(e), pl.ds(begin, end - begin)], rows.at[dy, m, span(e), to],
             rows_s.at[up, m, rel, e], rows_r.at[dy, m, rel, e], target,
         )
 
@@ -85,12 +86,12 @@
     def rows_over(m, e):
         return remote(mine.at[1, m, span(e)], rows.at[0, m, span(e), lanes(1)], rows_sib.at[m, e], rows_r.at[0, m, 1, e], sibling)
 
-    def cols_over(n):
-        half = pl.ds(0, ROWS)
-        return remote(cols.at[0, n, half, :], cols.at[0, n, pl.ds(ROWS, ROWS), :], cols_sib.at[n], cols_r.at[0, n, 1], sibling)
-
-    def cols_across(n):
-        half = pl.ds(0, ROWS)
+    def cols_over(n, begin=0, end=ROWS):
+        half, other = pl.ds(begin, end - begin), pl.ds(ROWS + begin, end - begin)
+        return remote(cols.at[0, n, half, :], cols.at[0, n, other, :], cols_sib.at[n], cols_r.at[0, n, 1], sibling)
+
+    def cols_across(n, begin=0, end=ROWS):
+        half = pl.ds(begin, end - begin)
         return remote(cols.at[0, n, half, :], cols.at[1, n, half, :], cols_s.at[n], cols_r.at[1, n, 0], across)
 
     def cols_on(n):
@@ -114,20 +115,27 @@
         )
 
     def z_home(m, c, e=None):
-        sem = c if e is None else c + e
+        sem = step_of(c, e)
         return remote(leaving.at[0, m, c, span(e)], landed.at[0, m, c, span(e)], z_s.at[0, m, sem], z_r.at[0, m, sem], beside)
 
-    def z_add(c):
-        return remote(leaving.at[1, 0, c], landed.at[1, 0, c], z_s.at[1, 0, c], z_r.at[1, 0, c], beside)
-
-    def z_on(m, c):
-        return remote(leaving.at[1, m, c], landed.at[0, m, c], z_s.at[1, m, c], z_r.at[0, m, c], corner)
-
-    def z_via(c):
-        return remote(leaving.at[1, 1, c], passing.at[c], z_s.at[1, 1, c], z_r.at[1, 1, c], corner)
-
-    def z_fwd(c):
-        return remote(passing.at[c], landed.at[1, 1, c], z_fs.at[c], z_fr.at[c], beside)
+    def step_of(c, e):
+        return c if e is None else c + e
+
+    def z_add(c, e=None):
+        sem, at = step_of(c, e), span(e)
+        return remote(leaving.at[1, 0, c, at], landed.at[1, 0, c, at], z_s.at[1, 0, sem], z_r.at[1, 0, sem], beside)
+
+    def z_on(m, c, e=None):
+        sem, at = step_of(c, e), span(e)
+        return remote(leaving.at[1, m, c, at], landed.at[0, m, c, at], z_s.at[1, m, sem], z_r.at[0, m, sem], corner)
+
+    def z_via(c, e=None):
+        sem, at = step_of(c, e), span(e)
+        return remote(leaving.at[1, 1, c, at], passing.at[c, at], z_s.at[1, 1, sem], z_r.at[1, 1, sem], corner)
+
+    def z_fwd(c, e=None):
+        sem, at = step_of(c, e), span(e)
+        return remote(passing.at[c, at], landed.at[1, 1, c, at], z_fs.at[sem], z_fr.at[sem], beside)
 
     def rhs_to(step):
         peer = (p, (o + step) % 16)
@@ -149,16 +157,11 @@
         block = jnp.broadcast_to(weight_row[0:1, r * 128 : (r + 1) * 128], (128, 128))
         wcol[pl.ds(r * 128, 128), :] = block.T
 
-    def widen(i, _):
-        at = pl.multiple_of(i * 128, 128)
-        ext[pl.ds(8, ROWS), pl.ds(at, 128)] = design[:, pl.ds(at, 128)].astype(F32)
-        return 0
-
-    incoming.wait()
-    lax.fori_loop(0, COLS // 128, widen, 0)
+    def order(i):
+        return i // 4, i % 2, 1 - (i // 2) % 2
 
     def filter_rows(i, r):
-        e, m, rel = i // 4, (i // 2) % 2, 1 - i % 2
+        e, m, rel = order(i)
         core = (k + rel) % 2
         at = pl.ds(pl.multiple_of(core * 512 + m * PART + e * 128, 128), 128)
         quarter = pl.ds(pl.multiple_of((core * 2 + m) * 128, 128), 128)
@@ -176,11 +179,15 @@
             rows[0, m, span(e), pl.ds(first, 128)] = turned
 
     def filter_later_rows(i, _):
+        e, m, rel = order(i)
+        at = pl.ds(pl.multiple_of((k + rel) % 2 * 512 + m * PART + e * 128, 128), 128)
+        ext[pl.ds(8, ROWS), at] = design[:, at].astype(F32)
         for r in range(1, ROWS // 128):
             filter_rows(i, r)
         return 0
 
-    lax.fori_loop(0, 4, filter_later_rows, 0)
+    incoming.wait()
+    lax.fori_loop(0, 2, filter_later_rows, 0)
     pl.semaphore_wait(barrier, len(greeted))
 
     @pl.when(o < 15)
@@ -188,6 +195,19 @@
         for copy in halo_copies():
             copy.start()
 
+    def start_early(i, _):
+        e, m, rel = order(i)
+        rows_out(m, rel, 0, 1 - m, 128).start()
+        return 0
+
+    def filter_and_start(i, _):
+        filter_later_rows(i, _)
+        return start_early(i, _)
+
+    lax.fori_loop(0, 2, start_early, 0)
+    lax.fori_loop(2, 4, filter_and_start, 0)
+    cols_across(0, 128).start()
+    cols_over(0, 128).start()
     lax.fori_loop(4, 8, filter_later_rows, 0)
 
     @pl.when(o > 0)
@@ -216,9 +236,16 @@
                 rows_at(dy, m, rel, e).wait_recv()
 
     def filter_block(i, _):
-        e, m, rel = i // 4, (i // 2) % 2, 1 - i % 2
+        e, m, rel = order(i)
         filter_rows(i, 0)
-        rows_out(m, rel, e, 1 - m).start()
+
+        @pl.when(e == 0)
+        def _():
+            rows_out(m, rel, e, 1 - m, 0, 128).start()
+
+        @pl.when(e == 1)
+        def _():
+            rows_out(m, rel, e, 1 - m).start()
 
         @pl.when(rel == 1)
         def _():
@@ -226,14 +253,14 @@
 
         @pl.when(i == 3)
         def _():
-            cols_over(0).start()
-            cols_across(0).start()
+            cols_across(0, 0, 128).start()
+            cols_over(0, 0, 128).start()
 
         return 0
 
     lax.fori_loop(0, 8, filter_block, 0)
+    cols_across(1).start()
     cols_over(1).start()
-    cols_across(1).start()
     first_far = near == 2
 
     @pl.when(first_far)
@@ -268,17 +295,18 @@
         def _():
             x_raw(role // 2, q, e).start()
 
-    def add_far(d, q, valid=True):
+    def add_far(d, q, valid=True, halves=None):
         @pl.when(valid)
         def _():
-            x_far(d, q).wait_recv()
-            for e in halves_of(q):
+            if halves is None or 0 in halves:
+                x_far(d, q).wait_recv()
+            for e in halves_of(q) if halves is None else halves:
                 both = part[2 * d, d, q, span(e)].astype(F32) + far[d, q, span(e)].astype(F32)
                 part[2 * d, d, q, span(e)] = both.astype(BF16)
                 x_sum(d, q, e).start()
 
     def halves_of(q):
-        return (0, 1) if isinstance(q, int) and q == 1 else (None,)
+        return (0, 1) if isinstance(q, int) and q % 2 == 1 else (None,)
 
     def by_near(*values):
         chosen = values[3]
@@ -354,43 +382,50 @@
     cols_on(1).start()
     cols_on(1).wait_recv()
 
-    def last_sums(q, valid=True):
-        add_far(by_near(0, 1, 0, 0), q, valid)
-        add_far(1, q, jnp.logical_and(valid, (near % 2) == 0))
+    def last_sums(q, valid=True, halves=None):
+        add_far(by_near(0, 1, 0, 0), q, valid, halves)
+        add_far(1, q, jnp.logical_and(valid, (near % 2) == 0), halves)
 
     multiply(by_near(2, 1, 0, 3), by_near(0, 0, 1, 1), 3)
     multiply(by_near(2, 1, 0, 3), by_near(1, 1, 0, 0), 3)
+
+    @pl.when(near != 0)
+    def _():
+        multiply(*third, 1)
+
     add_far(by_near(0, 0, 0, 1), 2, near != 0)
     add_far(1, 2, near == 2)
     multiply(by_near(3, 0, 3, 0), by_near(0, 0, 0, 1), 3)
     multiply(by_near(1, 0, 1, 0), by_near(1, 1, 1, 0), 3)
 
-    @pl.when(near != 0)
-    def _():
-        multiply(*third, 1)
-        multiply(*fourth, 1)
-
-    multiply(by_near(0, 2, 2, 2), by_near(0, 0, 0, 1), 3)
-    multiply(by_near(0, 3, 2, 1), by_near(1, 0, 1, 1), 3)
     for piece in (fifth, sixth):
         arrived(*piece)
     for q in (0, 2):
         for piece in (fifth, sixth):
             multiply(*piece, q)
         last_sums(q, near != 2)
+
+    @pl.when(near == 0)
+    def _():
+        multiply(*third, 1)
+
+    multiply(*fourth, 1)
+    multiply(by_near(0, 2, 2, 2), by_near(0, 0, 0, 1), 3)
+    multiply(by_near(0, 3, 2, 1), by_near(1, 0, 1, 1), 3)
     add_far(by_near(0, 0, 0, 1), 3, (near % 2) == 1)
     for piece in (fifth, sixth):
         multiply(*piece, 3)
-
-    @pl.when(near == 0)
-    def _():
-        multiply(*third, 1)
-        multiply(*fourth, 1)
-
-    last_sums(3)
+    last_sums(3, near == 2)
+    last_sums(3, near != 2, (0,))
     for piece in (fifth, sixth):
         multiply(*piece, 1)
-    last_sums(1, near == 0)
+
+    def final_sums(valid):
+        last_sums(1, valid, (0,))
+        last_sums(3, valid, (1,))
+        last_sums(1, valid, (1,))
+
+    final_sums(near == 0)
 
     for step in range(1, 16):
         rhs_to(step).wait_recv()
@@ -405,56 +440,58 @@
             x_raw(1 - m, q).wait_recv()
         return own[m, q, span(e)] + taken[0, m, q, span(e)].astype(F32) + taken[1, m, q, span(e)].astype(F32)
 
-    def keep_near(c):
-        for e in halves_of(c):
-            for m in range(2):
-                total = summed(m, c, e)
-
-                @pl.when(settled)
-                def _():
-                    own[m, c, span(e)] = total
-
-                @pl.when(jnp.logical_not(settled))
-                def _():
-                    leaving[0, m, c, span(e)] = total.astype(BF16)
-                    z_home(m, c, e).start()
-
-    def pass_over(c):
+    def keep_near(c, e=None):
+        for m in range(2):
+            total = summed(m, c, e)
+
+            @pl.when(settled)
+            def _():
+                own[m, c, span(e)] = total
+
+            @pl.when(jnp.logical_not(settled))
+            def _():
+                leaving[0, m, c, span(e)] = total.astype(BF16)
+                z_home(m, c, e).start()
+
+    def pass_over(c, e=None):
         for m in (1, 0):
-            total = summed(m, 2 + c)
+            total = summed(m, 2 + c, e)
 
             @pl.when(settled)
             def _():
-                leaving[1, m, c] = total.astype(BF16)
-                (z_add(c) if m == 0 else z_via(c)).start()
+                leaving[1, m, c, span(e)] = total.astype(BF16)
+                (z_add(c, e) if m == 0 else z_via(c, e)).start()
 
             @pl.when(jnp.logical_not(settled))
             def _():
                 if m == 0:
-                    own[m, 2 + c] = total
+                    own[m, 2 + c, span(e)] = total
                 else:
-                    leaving[1, m, c] = total.astype(BF16)
-                    z_on(m, c).start()
-
-    def pass_on(c):
+                    leaving[1, m, c, span(e)] = total.astype(BF16)
+                    z_on(m, c, e).start()
+
+    def pass_on(c, e=None):
         @pl.when(settled)
         def _():
-            z_via(c).wait_recv()
-            z_fwd(c).start()
+            z_via(c, e).wait_recv()
+            z_fwd(c, e).start()
 
         @pl.when(jnp.logical_not(settled))
         def _():
-            z_add(c).wait_recv()
-            leaving[1, 0, c] = (own[0, 2 + c] + landed[1, 0, c].astype(F32)).astype(BF16)
-            z_on(0, c).start()
+            z_add(c, e).wait_recv()
+            leaving[1, 0, c, span(e)] = (own[0, 2 + c, span(e)] + landed[1, 0, c, span(e)].astype(F32)).astype(BF16)
+            z_on(0, c, e).start()
 
     keep_near(0)
     pass_over(0)
-    last_sums(1, (near % 2) == 1)
-    pass_over(1)
+    final_sums((near % 2) == 1)
     pass_on(0)
-    keep_near(1)
-    pass_on(1)
+    pass_over(1, 0)
+    keep_near(1, 0)
+    pass_on(1, 0)
+    pass_over(1, 1)
+    keep_near(1, 1)
+    pass_on(1, 1)
 
     def place(m, c, total):
         for b in range(4):
@@ -472,10 +509,12 @@
 
             @pl.when(jnp.logical_not(settled))
             def _():
-                z_on(m, c).wait_recv()
+                for e in halves_of(c):
+                    z_on(m, c, e).wait_recv()
                 total = landed[0, m, c].astype(F32)
                 if m == 1:
-                    z_fwd(c).wait_recv()
+                    for e in halves_of(c):
+                        z_fwd(c, e).wait_recv()
                     total = total + landed[1, 1, c].astype(F32)
                 place(m, c, total)
 
@@ -491,7 +530,8 @@
         cols_across(m).wait_send()
         cols_on(m).wait_send()
         for c in range(2):
-            z_on(m, c).wait_send()
+            for e in halves_of(c):
+                z_on(m, c, e).wait_send()
 
             @pl.when(jnp.logical_not(settled))
             def _():
@@ -500,7 +540,8 @@
 
         @pl.when(settled)
         def _():
-            z_fwd(m).wait_send()
+            for e in halves_of(m):
+                z_fwd(m, e).wait_send()
 
         for q in range(4):
             x_far(m, q).wait_send()
@@ -549,7 +590,7 @@
             dma((2, 2, 2, 2)), dma((2, 2, 2)), dma((2, 2)), dma((4, 2, 2, 2)),
             dma((2,)), dma((2,)), dma((2,)), dma((2, 2, 2)),
             dma((2, 4, 4)), dma((2, 4, 4)),
-            dma((2, 2, 3)), dma((2, 2, 3)), dma((2,)), dma((2,)),
+            dma((2, 2, 3)), dma((2, 2, 3)), dma((3,)), dma((3,)),
             dma((16,)), dma((16,)),
         ],
         compiler_params=pltpu.CompilerParams(collective_id=0, has_side_effects=True, vmem_limit_bytes=60 << 20),

time: 115 us -> 110 us (0.957)
  the two profiles are of different devices: /device:TPU:80 before, /device:TPU:74 now
where the time goes in v4:
time: 110 us
  Pallas kernels  105 us (95%)
  local copies, waits for them, and re-layouts  4.36 us (4%)
    pallas_call x1, Pallas kernels, per_device(): pl.pallas_call(functools.partial(kernel, 1.0 / total_rows, 1.0 / math.sqr...  105 us
    unnamed x7, local copies, waits for them, and re-layouts  4.36 us

profile of v4, /device:TPU:74, one launch (start us, length us, event | category | flops | bytes accessed | tf_op | source)
XLA Modules:
  0.0 110.0 jit_solution(13417610245310376225)
XLA Ops:
  0.6 105.0 %normal_equations.1 = (f32[512,1024]{1,0:T(8,128)}, f32[1024]{0:T(1024)}, f32[640]{0:T(1024)}) custom-call(bf16[640,1024]{1,0:T(8,128)(2,1)} %design_hbm.1, bf16[640]{0:T(1024)(128)(2,1)} %observed.1, f32[640]{0:T(1024)} %weight.1, f32[7]{0:T(128)} %taps.1), custom_call_target="tpu_custom_call" | custom-call | tf_op jit(solution)/shard_map/normal_equations/pallas_call | solution.py:561
  105.7 0.0 copy-start.1
  105.7 0.0 copy-start
  105.7 3.2 %copy.10 = f32[512,1024]{1,0:T(8,128)} copy(f32[512,1024]{1,0:T(8,128)} %get-tuple-element.6) | data formatting | bytes 4194304
  108.8 0.0 copy-done.1
  108.8 0.6 copy.11
  109.4 0.0 copy-done
  109.4 0.6 copy.12
Async XLA Ops:
  105.7 3.2 %copy-start.1 = (f32[1024]{0:T(1024)S(1)}, f32[1024]{0:T(1024)}, u32[]{:S(2)}) copy-start(f32[1024]{0:T(1024)} %get-tuple-element.7) | copy-start | bytes 12292
  105.7 3.8 %copy-start = (f32[640]{0:T(1024)S(1)}, f32[640]{0:T(1024)}, u32[]{:S(2)}) copy-start(f32[640]{0:T(1024)} %get-tuple-element.8) | copy-start | bytes 7684

commit v5 on v4

--- a/solution.py
+++ b/solution.py
@@ -21,15 +21,16 @@
     scale, rhs_scale,
     design_hbm, observed, weight, taps,
     normal, rhs, filtered_obs,
-    design, ext, halo, obs_tail, obs_halo, wcol, mine, weighted, rows, cols, part, own, taken, far,
+    design, ext, halo, obs_tail, obs_halo, wcol, mine, weighted, rows, cols, part, own, taken, far, giving, swapped,
     leaving, landed, passing, rhs_all,
-    design_s, halo_s, halo_r, rows_s, rows_f, rows_sib, rows_r, cols_s, cols_sib, cols_f, cols_r, x_s, x_r, z_s, z_r, z_fs, z_fr, rhs_s, rhs_r,
+    design_s, halo_s, halo_r, rows_s, rows_f, rows_sib, rows_r, cols_s, cols_sib, cols_f, cols_r, x_s, x_r, swap_s, swap_r, z_s, z_r, z_fs, z_fr, rhs_s, rhs_r,
 ):
     p, o = lax.axis_index("param"), lax.axis_index("obs")
     y, h = p // 2, p % 2
     x, l, k = o // 4, (o // 2) % 2, o % 2
     near = (y - x + 4) % 4
     settled = l == h
+    kept, given = jnp.where(settled, 1, 3), jnp.where(settled, 3, 1)
 
     def param_of(y_, h_):
         return ((y_ + 4) % 4) * 2 + h_
@@ -101,18 +102,25 @@
     def beyond(d):
         return (p, obs_of(x + 1 - 2 * d, l, k))
 
-    def x_far(d, q, e=None):
-        return remote(part.at[1, d, q, span(e)], far.at[d, q, span(e)], x_s.at[d, 0, q], x_r.at[d, 0, q], beyond(d))
-
-    def x_raw(d, q, e=None):
-        dst = taken.at[d, 1 - d, q, span(e)]
-        return remote(part.at[2 * d, 1 - d, q, span(e)], dst, x_s.at[d, 1, q], x_r.at[d, 1, q], beyond(d))
-
-    def x_sum(d, q, e=None):
-        kind = 2 if e is None else 2 + e
-        return remote(
-            part.at[2 * d, d, q, span(e)], taken.at[d, d, q, span(e)], x_s.at[d, kind, q], x_r.at[d, kind, q], beyond(d)
-        )
+    def x_far(d, q, e=None, late=0):
+        at = span(e)
+        return remote(part.at[1, d, q, at], far.at[d, q, at], x_s.at[d, 3 * late, q], x_r.at[d, 3 * late, q], beyond(d))
+
+    def x_raw(d, q, e=None, late=0):
+        at, kind = span(e), 1 + 3 * late
+        dst = taken.at[d, 1 - d, q, at]
+        return remote(part.at[2 * d, 1 - d, q, at], dst, x_s.at[d, kind, q], x_r.at[d, kind, q], beyond(d))
+
+    def x_sum(d, q, e=None, late=0):
+        at, kind = span(e), 2 + 3 * late
+        return remote(part.at[2 * d, d, q, at], taken.at[d, d, q, at], x_s.at[d, kind, q], x_r.at[d, kind, q], beyond(d))
+
+    def swap(role, m):
+        place = part.at[role - 1, m, given, span(1)]
+        return remote(place, swapped.at[role, m], swap_s.at[role, m], swap_r.at[role, m], beside)
+
+    def swap_own(m):
+        return remote(giving.at[m], swapped.at[0, m], swap_s.at[0, m], swap_r.at[0, m], beside)
 
     def z_home(m, c, e=None):
         sem = step_of(c, e)
@@ -287,26 +295,67 @@
 
         lax.fori_loop(0, 2, chunk, 0)
 
+        if q % 2 == 1 and e == 1:
+            return
+        e = 0 if q % 2 == 1 else e
+
         @pl.when(role == 2)
         def _():
             x_far(m, q, e).start()
 
-        @pl.when(jnp.logical_or(jnp.logical_and(role == 1, m == 1), jnp.logical_and(role == 3, m == 0)))
+        @pl.when(as_it_is(role, m))
         def _():
             x_raw(role // 2, q, e).start()
 
-    def add_far(d, q, valid=True, halves=None):
+    def as_it_is(role, m):
+        return jnp.logical_or(jnp.logical_and(role == 1, m == 1), jnp.logical_and(role == 3, m == 0))
+
+    def give(dy, m):
+        role = (near + dy) % 4
+
+        @pl.when(role == 0)
+        def _():
+            giving[m] = own[m, given, span(1)].astype(BF16)
+            swap_own(m).start()
+
+        @pl.when(role != 0)
+        def _():
+            swap(role, m).start()
+
+    def take(dy, m):
+        role = (near + dy) % 4
+
+        @pl.when(role == 0)
+        def _():
+            swap_own(m).wait_recv()
+            own[m, kept, span(1)] = own[m, kept, span(1)] + swapped[0, m].astype(F32)
+
+        @pl.when(role != 0)
+        def _():
+            swap(role, m).wait_recv()
+            both = part[role - 1, m, kept, span(1)].astype(F32) + swapped[role, m].astype(F32)
+            part[role - 1, m, kept, span(1)] = both.astype(BF16)
+
+        @pl.when(role == 2)
+        def _():
+            x_far(m, kept, 1, 1).start()
+
+        @pl.when(as_it_is(role, m))
+        def _():
+            x_raw(role // 2, kept, 1, 1).start()
+
+    def add_far(d, q, valid=True, late=0):
+        e = late if late else first_of(q)
+
         @pl.when(valid)
         def _():
-            if halves is None or 0 in halves:
-                x_far(d, q).wait_recv()
-            for e in halves_of(q) if halves is None else halves:
-                both = part[2 * d, d, q, span(e)].astype(F32) + far[d, q, span(e)].astype(F32)
-                part[2 * d, d, q, span(e)] = both.astype(BF16)
-                x_sum(d, q, e).start()
-
-    def halves_of(q):
-        return (0, 1) if isinstance(q, int) and q % 2 == 1 else (None,)
+            x_far(d, q, e, late).wait_recv()
+            both = part[2 * d, d, q, span(e)].astype(F32) + far[d, q, span(e)].astype(F32)
+            part[2 * d, d, q, span(e)] = both.astype(BF16)
+            x_sum(d, q, e, late).start()
+
+    def first_of(q):
+        return 0 if q % 2 == 1 else None
 
     def by_near(*values):
         chosen = values[3]
@@ -373,59 +422,114 @@
     fifth = (by_near(1, 2, 1, 2), by_near(0, 1, 0, 0))
     sixth = (by_near(3, 3, 3, 1), by_near(1, 1, 1, 0))
     arrived(*third)
-    multiply(*third, 0)
+    multiply(*third, 2)
     arrived(*fourth)
-    multiply(*fourth, 0)
-    multiply(*third, 2)
     multiply(*fourth, 2)
+    for q in (0, 1):
+        multiply(*third, q)
+        multiply(*fourth, q)
     cols_across(1).wait_recv()
     cols_on(1).start()
     cols_on(1).wait_recv()
 
-    def last_sums(q, valid=True, halves=None):
-        add_far(by_near(0, 1, 0, 0), q, valid, halves)
-        add_far(1, q, jnp.logical_and(valid, (near % 2) == 0), halves)
-
-    multiply(by_near(2, 1, 0, 3), by_near(0, 0, 1, 1), 3)
-    multiply(by_near(2, 1, 0, 3), by_near(1, 1, 0, 0), 3)
-
-    @pl.when(near != 0)
-    def _():
-        multiply(*third, 1)
-
+    def last_sums(q, valid=True):
+        add_far(by_near(0, 1, 0, 0), q, valid)
+        add_far(1, q, jnp.logical_and(valid, (near % 2) == 0))
+
+    slots = (
+        (by_near(2, 1, 0, 3), by_near(0, 0, 1, 1)),
+        (by_near(2, 1, 0, 3), by_near(1, 1, 0, 0)),
+        (by_near(3, 0, 3, 0), by_near(0, 0, 0, 1)),
+        (by_near(1, 0, 1, 0), by_near(1, 1, 1, 0)),
+        (by_near(0, 2, 2, 2), by_near(0, 0, 0, 1)),
+        (by_near(0, 3, 2, 1), by_near(1, 0, 1, 1)),
+    )
+    def summed(m, q, e=None, late=0):
+        x_sum(m, q, e, late).wait_recv()
+        x_raw(1 - m, q, e, late).wait_recv()
+        return own[m, q, span(e)] + taken[0, m, q, span(e)].astype(F32) + taken[1, m, q, span(e)].astype(F32)
+
+    def keep_near(c, e=None):
+        for m in range(2):
+            total = summed(m, c, e)
+
+            @pl.when(settled)
+            def _():
+                own[m, c, span(e)] = total
+
+            @pl.when(jnp.logical_not(settled))
+            def _():
+                leaving[0, m, c, span(e)] = total.astype(BF16)
+                z_home(m, c, e).start()
+
+    def pass_over(c, e=None):
+        for m in (1, 0):
+            total = summed(m, 2 + c, e)
+
+            @pl.when(settled)
+            def _():
+                leaving[1, m, c, span(e)] = total.astype(BF16)
+                (z_add(c, e) if m == 0 else z_via(c, e)).start()
+
+            @pl.when(jnp.logical_not(settled))
+            def _():
+                if m == 0:
+                    own[m, 2 + c, span(e)] = total
+                else:
+                    leaving[1, m, c, span(e)] = total.astype(BF16)
+                    z_on(m, c, e).start()
+
+    def hand_on(c, e=None):
+        @pl.when(settled)
+        def _():
+            z_via(c, e).wait_recv()
+            z_fwd(c, e).start()
+
+    def add_on(c, e=None):
+        @pl.when(jnp.logical_not(settled))
+        def _():
+            z_add(c, e).wait_recv()
+            leaving[1, 0, c, span(e)] = (own[0, 2 + c, span(e)] + landed[1, 0, c, span(e)].astype(F32)).astype(BF16)
+            z_on(0, c, e).start()
+
+    def late_sums(valid):
+        for d in range(2):
+            add_far(d, kept, valid, 1)
+
+    for slot in slots[0:2]:
+        multiply(*slot, 3)
+        give(*slot)
     add_far(by_near(0, 0, 0, 1), 2, near != 0)
     add_far(1, 2, near == 2)
-    multiply(by_near(3, 0, 3, 0), by_near(0, 0, 0, 1), 3)
-    multiply(by_near(1, 0, 1, 0), by_near(1, 1, 1, 0), 3)
-
+    for slot in slots[2:6]:
+        multiply(*slot, 3)
+        give(*slot)
     for piece in (fifth, sixth):
         arrived(*piece)
-    for q in (0, 2):
-        for piece in (fifth, sixth):
-            multiply(*piece, q)
-        last_sums(q, near != 2)
-
-    @pl.when(near == 0)
-    def _():
-        multiply(*third, 1)
-
-    multiply(*fourth, 1)
-    multiply(by_near(0, 2, 2, 2), by_near(0, 0, 0, 1), 3)
-    multiply(by_near(0, 3, 2, 1), by_near(1, 0, 1, 1), 3)
+    for piece in (fifth, sixth):
+        multiply(*piece, 2)
+    last_sums(2, near != 2)
+    for slot in slots[0:2]:
+        take(*slot)
+    for piece in (fifth, sixth):
+        multiply(*piece, 0)
+    last_sums(0, near != 2)
     add_far(by_near(0, 0, 0, 1), 3, (near % 2) == 1)
     for piece in (fifth, sixth):
         multiply(*piece, 3)
-    last_sums(3, near == 2)
-    last_sums(3, near != 2, (0,))
-    for piece in (fifth, sixth):
         multiply(*piece, 1)
-
-    def final_sums(valid):
-        last_sums(1, valid, (0,))
-        last_sums(3, valid, (1,))
-        last_sums(1, valid, (1,))
-
-    final_sums(near == 0)
+        give(*piece)
+    for slot in slots[2:4]:
+        take(*slot)
+    last_sums(3)
+    last_sums(1, near == 0)
+
+    @pl.when(near == 0)
+    def _():
+        pass_over(0)
+
+    for slot in slots[4:6] + (fifth, sixth):
+        take(*slot)
 
     for step in range(1, 16):
         rhs_to(step).wait_recv()
@@ -434,89 +538,57 @@
         total = total + rhs_all[step]
     rhs[...] = (total * rhs_scale).reshape(COLS)
 
-    def summed(m, q, e=None):
-        x_sum(m, q, e).wait_recv()
-        if not e:
-            x_raw(1 - m, q).wait_recv()
-        return own[m, q, span(e)] + taken[0, m, q, span(e)].astype(F32) + taken[1, m, q, span(e)].astype(F32)
-
-    def keep_near(c, e=None):
-        for m in range(2):
-            total = summed(m, c, e)
-
-            @pl.when(settled)
-            def _():
-                own[m, c, span(e)] = total
-
-            @pl.when(jnp.logical_not(settled))
-            def _():
-                leaving[0, m, c, span(e)] = total.astype(BF16)
-                z_home(m, c, e).start()
-
-    def pass_over(c, e=None):
-        for m in (1, 0):
-            total = summed(m, 2 + c, e)
-
-            @pl.when(settled)
-            def _():
-                leaving[1, m, c, span(e)] = total.astype(BF16)
-                (z_add(c, e) if m == 0 else z_via(c, e)).start()
-
-            @pl.when(jnp.logical_not(settled))
-            def _():
-                if m == 0:
-                    own[m, 2 + c, span(e)] = total
-                else:
-                    leaving[1, m, c, span(e)] = total.astype(BF16)
-                    z_on(m, c, e).start()
-
-    def pass_on(c, e=None):
+    late_sums((near % 2) == 0)
+    @pl.when(near != 0)
+    def _():
+        pass_over(0)
+
+    keep_near(0)
+    last_sums(1, (near % 2) == 1)
+    late_sums((near % 2) == 1)
+    add_on(0)
+    pass_over(1, 0)
+    hand_on(0)
+    keep_near(1, 0)
+    add_on(1, 0)
+    hand_on(1, 0)
+    for m in range(2):
+        total = summed(m, kept, 1, 1)
+
         @pl.when(settled)
         def _():
-            z_via(c, e).wait_recv()
-            z_fwd(c, e).start()
+            own[m, 1, span(1)] = total
 
         @pl.when(jnp.logical_not(settled))
         def _():
-            z_add(c, e).wait_recv()
-            leaving[1, 0, c, span(e)] = (own[0, 2 + c, span(e)] + landed[1, 0, c, span(e)].astype(F32)).astype(BF16)
-            z_on(0, c, e).start()
-
-    keep_near(0)
-    pass_over(0)
-    final_sums((near % 2) == 1)
-    pass_on(0)
-    pass_over(1, 0)
-    keep_near(1, 0)
-    pass_on(1, 0)
-    pass_over(1, 1)
-    keep_near(1, 1)
-    pass_on(1, 1)
-
-    def place(m, c, total):
+            leaving[1, m, 1, span(1)] = total.astype(BF16)
+            z_on(m, 1, 1).start()
+
+    def place(m, c, e, total):
+        first, count = m * PART + (128 if e == 1 else 0), PART if e is None else 128
         for b in range(4):
             to = pl.ds(b // 2 * 512 + b % 2 * 256 + c * 128, 128)
-            normal[pl.ds(m * PART, PART), to] = total[:, b * 128 : b * 128 + 128] * scale
-
-    for c in range(2):
+            normal[pl.ds(first, count), to] = total[:, b * 128 : b * 128 + 128] * scale
+
+    for c, e in ((0, None), (1, 0), (1, 1)):
         for m in range(2):
 
             @pl.when(settled)
             def _():
-                for e in halves_of(c):
+                total = own[m, c, span(e)]
+                if e != 1:
                     z_home(m, c, e).wait_recv()
-                place(m, c, own[m, c] + landed[0, m, c].astype(F32))
+                    total = total + landed[0, m, c, span(e)].astype(F32)
+                place(m, c, e, total)
 
             @pl.when(jnp.logical_not(settled))
             def _():
-                for e in halves_of(c):
-                    z_on(m, c, e).wait_recv()
-                total = landed[0, m, c].astype(F32)
-                if m == 1:
-                    for e in halves_of(c):
-                        z_fwd(c, e).wait_recv()
-                    total = total + landed[1, 1, c].astype(F32)
-                place(m, c, total)
+                z_on(m, c, e).wait_recv()
+                total = landed[0, m, c, span(e)].astype(F32)
+                if m == 1 and e != 1:
+                    z_fwd(c, e).wait_recv()
+                    total = total + landed[1, 1, c, span(e)].astype(F32)
+                place(m, c, e, total)
 
     @pl.when(o < 15)
     def _():
@@ -529,25 +601,29 @@
         cols_over(m).wait_send()
         cols_across(m).wait_send()
         cols_on(m).wait_send()
-        for c in range(2):
-            for e in halves_of(c):
-                z_on(m, c, e).wait_send()
-
-            @pl.when(jnp.logical_not(settled))
-            def _():
-                for e in halves_of(c):
-                    z_home(m, c, e).wait_send()
+        z_on(m, 0).wait_send()
+        z_on(m, 1, 0).wait_send()
+        swap_own(m).wait_send()
+        for role in range(1, 4):
+            swap(role, m).wait_send()
 
         @pl.when(settled)
         def _():
-            for e in halves_of(m):
-                z_fwd(m, e).wait_send()
+            z_fwd(m, first_of(m)).wait_send()
+
+        @pl.when(jnp.logical_not(settled))
+        def _():
+            z_on(m, 1, 1).wait_send()
+            z_home(m, 0).wait_send()
+            z_home(m, 1, 0).wait_send()
 
         for q in range(4):
-            x_far(m, q).wait_send()
-            x_raw(m, q).wait_send()
-            for e in halves_of(q):
-                x_sum(m, q, e).wait_send()
+            x_far(m, q, first_of(q)).wait_send()
+            x_raw(m, q, first_of(q)).wait_send()
+            x_sum(m, q, first_of(q)).wait_send()
+        x_far(m, kept, 1, 1).wait_send()
+        x_raw(m, kept, 1, 1).wait_send()
+        x_sum(m, kept, 1, 1).wait_send()
     for copy in first_pieces() + passed_on() + second_pieces():
         copy.wait_send()
     for step in range(1, 16):
@@ -582,6 +658,8 @@
             pltpu.VMEM((2, 4, PART, 512), F32),
             pltpu.VMEM((2, 2, 4, PART, 512), BF16),
             pltpu.VMEM((2, 4, PART, 512), BF16),
+            pltpu.VMEM((2, 128, 512), BF16),
+            pltpu.VMEM((4, 2, 128, 512), BF16),
             pltpu.VMEM((2, 2, 2, PART, 512), BF16),
             pltpu.VMEM((2, 2, 2, PART, 512), BF16),
             pltpu.VMEM((2, PART, 512), BF16),
@@ -589,7 +667,7 @@
             dma, dma((2,)), dma((2,)),
             dma((2, 2, 2, 2)), dma((2, 2, 2)), dma((2, 2)), dma((4, 2, 2, 2)),
             dma((2,)), dma((2,)), dma((2,)), dma((2, 2, 2)),
-            dma((2, 4, 4)), dma((2, 4, 4)),
+            dma((2, 6, 4)), dma((2, 6, 4)), dma((4, 2)), dma((4, 2)),
             dma((2, 2, 3)), dma((2, 2, 3)), dma((3,)), dma((3,)),
             dma((16,)), dma((16,)),
         ],

time: 110 us -> 105 us (0.955)
  the two profiles are of different devices: /device:TPU:74 before, /device:TPU:34 now
where the time goes in v5:
time: 105 us; the launch traced here: 104 us
  Pallas kernels  99.4 us (95%)
  local copies, waits for them, and re-layouts  4.36 us (4%)
    pallas_call x1, Pallas kernels, per_device(): pl.pallas_call(functools.partial(kernel, 1.0 / total_rows, 1.0 / math.sqr...  99.4 us
    unnamed x7, local copies, waits for them, and re-layouts  4.36 us

profile of v5, /device:TPU:34, one launch (start us, length us, event | category | flops | bytes accessed | tf_op | source)
XLA Modules:
  0.0 104.5 jit_solution(13763970036787120401)
XLA Ops:
  0.6 99.4 %normal_equations.1 = (f32[512,1024]{1,0:T(8,128)}, f32[1024]{0:T(1024)}, f32[640]{0:T(1024)}) custom-call(bf16[640,1024]{1,0:T(8,128)(2,1)} %design_hbm.1, bf16[640]{0:T(1024)(128)(2,1)} %observed.1, f32[640]{0:T(1024)} %weight.1, f32[7]{0:T(128)} %taps.1), custom_call_target="tpu_custom_call" | custom-call | tf_op jit(solution)/shard_map/normal_equations/pallas_call | solution.py:637
  100.1 0.0 copy-start.1
  100.1 0.0 copy-start
  100.1 3.2 %copy.10 = f32[512,1024]{1,0:T(8,128)} copy(f32[512,1024]{1,0:T(8,128)} %get-tuple-element.6) | data formatting | bytes 4194304
  103.3 0.0 copy-done.1
  103.3 0.6 copy.11
  103.9 0.0 copy-done
  103.9 0.6 copy.12
Async XLA Ops:
  100.1 3.2 %copy-start.1 = (f32[1024]{0:T(1024)S(1)}, f32[1024]{0:T(1024)}, u32[]{:S(2)}) copy-start(f32[1024]{0:T(1024)} %get-tuple-element.7) | copy-start | bytes 12292
  100.1 3.8 %copy-start = (f32[640]{0:T(1024)S(1)}, f32[640]{0:T(1024)}, u32[]{:S(2)}) copy-start(f32[640]{0:T(1024)} %get-tuple-element.8) | copy-start | bytes 7684

commit v6 on v5

--- a/solution.py
+++ b/solution.py
@@ -22,8 +22,8 @@
     design_hbm, observed, weight, taps,
     normal, rhs, filtered_obs,
     design, ext, halo, obs_tail, obs_halo, wcol, mine, weighted, rows, cols, part, own, taken, far, giving, swapped,
-    leaving, landed, passing, rhs_all,
-    design_s, halo_s, halo_r, rows_s, rows_f, rows_sib, rows_r, cols_s, cols_sib, cols_f, cols_r, x_s, x_r, swap_s, swap_r, z_s, z_r, z_fs, z_fr, rhs_s, rhs_r,
+    leaving, landed, passing, result, small_obs, small_rhs, rhs_all,
+    design_s, out_s, small_s, halo_s, halo_r, rows_s, rows_f, rows_sib, rows_r, cols_s, cols_sib, cols_f, cols_r, x_s, x_r, swap_s, swap_r, z_s, z_r, z_fs, z_fr, rhs_s, rhs_r,
 ):
     p, o = lax.axis_index("param"), lax.axis_index("obs")
     y, h = p // 2, p % 2
@@ -144,6 +144,12 @@
     def z_fwd(c, e=None):
         sem, at = step_of(c, e), span(e)
         return remote(passing.at[c, at], landed.at[1, 1, c, at], z_fs.at[sem], z_fr.at[sem], beside)
+
+    def obs_out():
+        return pltpu.make_async_copy(small_obs, filtered_obs, small_s.at[0])
+
+    def rhs_out():
+        return pltpu.make_async_copy(small_rhs, rhs, small_s.at[1])
 
     def rhs_to(step):
         peer = (p, (o + step) % 16)
@@ -403,7 +409,8 @@
     total = signal_row
     for lag in range(1, LAGS + 1):
         total = total + taps[lag - 1] * pltpu.roll(extended, lag, 1)[:, 128:]
-    filtered_obs[...] = total[0:1, :].reshape(ROWS)
+    small_obs[...] = total[0:1, :].reshape(ROWS)
+    obs_out().start()
     weighted[...] = jnp.concatenate([weight_row * total, weight_row * total], axis=0).astype(BF16)
     line = lax.broadcasted_iota(jnp.int32, (8, 128), 0)
     sums = jnp.zeros((8, 128), F32)
@@ -536,7 +543,8 @@
     total = rhs_all[0]
     for step in range(1, 16):
         total = total + rhs_all[step]
-    rhs[...] = (total * rhs_scale).reshape(COLS)
+    small_rhs[...] = (total * rhs_scale).reshape(COLS)
+    rhs_out().start()
 
     late_sums((near % 2) == 0)
     @pl.when(near != 0)
@@ -564,32 +572,8 @@
             leaving[1, m, 1, span(1)] = total.astype(BF16)
             z_on(m, 1, 1).start()
 
-    def place(m, c, e, total):
-        first, count = m * PART + (128 if e == 1 else 0), PART if e is None else 128
-        for b in range(4):
-            to = pl.ds(b // 2 * 512 + b % 2 * 256 + c * 128, 128)
-            normal[pl.ds(first, count), to] = total[:, b * 128 : b * 128 + 128] * scale
-
-    for c, e in ((0, None), (1, 0), (1, 1)):
-        for m in range(2):
-
-            @pl.when(settled)
-            def _():
-                total = own[m, c, span(e)]
-                if e != 1:
-                    z_home(m, c, e).wait_recv()
-                    total = total + landed[0, m, c, span(e)].astype(F32)
-                place(m, c, e, total)
-
-            @pl.when(jnp.logical_not(settled))
-            def _():
-                z_on(m, c, e).wait_recv()
-                total = landed[0, m, c, span(e)].astype(F32)
-                if m == 1 and e != 1:
-                    z_fwd(c, e).wait_recv()
-                    total = total + landed[1, 1, c, span(e)].astype(F32)
-                place(m, c, e, total)
-
+    obs_out().wait()
+    rhs_out().wait()
     @pl.when(o < 15)
     def _():
         for copy in halo_copies():
@@ -601,22 +585,9 @@
         cols_over(m).wait_send()
         cols_across(m).wait_send()
         cols_on(m).wait_send()
-        z_on(m, 0).wait_send()
-        z_on(m, 1, 0).wait_send()
         swap_own(m).wait_send()
         for role in range(1, 4):
             swap(role, m).wait_send()
-
-        @pl.when(settled)
-        def _():
-            z_fwd(m, first_of(m)).wait_send()
-
-        @pl.when(jnp.logical_not(settled))
-        def _():
-            z_on(m, 1, 1).wait_send()
-            z_home(m, 0).wait_send()
-            z_home(m, 1, 0).wait_send()
-
         for q in range(4):
             x_far(m, q, first_of(q)).wait_send()
             x_raw(m, q, first_of(q)).wait_send()
@@ -628,6 +599,55 @@
         copy.wait_send()
     for step in range(1, 16):
         rhs_to(step).wait_send()
+
+    def place(m, c, e, total):
+        first, count = m * PART + (128 if e == 1 else 0), PART if e is None else 128
+        for b in range(4):
+            to = pl.ds(b // 2 * 512 + b % 2 * 256 + c * 128, 128)
+            result[pl.ds(first, count), to] = total[:, b * 128 : b * 128 + 128] * scale
+        if c == 1:
+            leave(m, e).start()
+
+    def leave(m, e):
+        half = pl.ds(m * PART + 128 * e, 128)
+        return pltpu.make_async_copy(result.at[half], normal.at[half], out_s.at[m, e])
+
+    for c, e in ((0, None), (1, 0), (1, 1)):
+        for m in range(2):
+
+            @pl.when(settled)
+            def _():
+                total = own[m, c, span(e)]
+                if e != 1:
+                    z_home(m, c, e).wait_recv()
+                    total = total + landed[0, m, c, span(e)].astype(F32)
+                place(m, c, e, total)
+
+            @pl.when(jnp.logical_not(settled))
+            def _():
+                z_on(m, c, e).wait_recv()
+                total = landed[0, m, c, span(e)].astype(F32)
+                if m == 1 and e != 1:
+                    z_fwd(c, e).wait_recv()
+                    total = total + landed[1, 1, c, span(e)].astype(F32)
+                place(m, c, e, total)
+
+    for m in range(2):
+        for e in range(2):
+            leave(m, e).wait()
+    for m in range(2):
+        z_on(m, 0).wait_send()
+        z_on(m, 1, 0).wait_send()
+
+        @pl.when(settled)
+        def _():
+            z_fwd(m, first_of(m)).wait_send()
+
+        @pl.when(jnp.logical_not(settled))
+        def _():
+            z_on(m, 1, 1).wait_send()
+            z_home(m, 0).wait_send()
+            z_home(m, 1, 0).wait_send()
 
 
 def per_device(design, observed, row_weight, taps):
@@ -642,7 +662,7 @@
             jax.ShapeDtypeStruct((ROWS,), F32),
         ),
         in_specs=[pl.BlockSpec(memory_space=pl.ANY), vmem, vmem, pl.BlockSpec(memory_space=pltpu.SMEM)],
-        out_specs=(vmem, vmem, vmem),
+        out_specs=(pl.BlockSpec(memory_space=pl.ANY),) * 3,
         scratch_shapes=[
             pltpu.VMEM((ROWS, COLS), BF16),
             pltpu.VMEM((ROWS + 8, COLS), F32),
@@ -663,8 +683,11 @@
             pltpu.VMEM((2, 2, 2, PART, 512), BF16),
             pltpu.VMEM((2, 2, 2, PART, 512), BF16),
             pltpu.VMEM((2, PART, 512), BF16),
+            pltpu.VMEM((512, COLS), F32),
+            pltpu.VMEM((ROWS,), F32),
+            pltpu.VMEM((COLS,), F32),
             pltpu.VMEM((16, 8, 128), F32),
-            dma, dma((2,)), dma((2,)),
+            dma, dma((2, 2)), dma((2,)), dma((2,)), dma((2,)),
             dma((2, 2, 2, 2)), dma((2, 2, 2)), dma((2, 2)), dma((4, 2, 2, 2)),
             dma((2,)), dma((2,)), dma((2,)), dma((2, 2, 2)),
             dma((2, 6, 4)), dma((2, 6, 4)), dma((4, 2)), dma((4, 2)),

time: 105 us -> 104 us (level)
  no operation moved by 1% of the time
where the time goes in v6:
time: 104 us
  Pallas kernels  98.8 us (95%)
  local copies, waits for them, and re-layouts  4.36 us (4%)
    pallas_call x1, Pallas kernels, per_device(): pl.pallas_call(functools.partial(kernel, 1.0 / total_rows, 1.0 / math.sqr...  98.8 us
    unnamed x7, local copies, waits for them, and re-layouts  4.36 us

profile of v6, /device:TPU:34, one launch (start us, length us, event | category | flops | bytes accessed | tf_op | source)
XLA Modules:
  0.0 103.8 jit_solution(9261407174833149056)
XLA Ops:
  0.6 98.8 %normal_equations.1 = (f32[512,1024]{1,0:T(8,128)}, f32[1024]{0:T(1024)}, f32[640]{0:T(1024)}) custom-call(bf16[640,1024]{1,0:T(8,128)(2,1)} %design_hbm.1, bf16[640]{0:T(1024)(128)(2,1)} %observed.1, f32[640]{0:T(1024)} %weight.1, f32[7]{0:T(128)} %taps.1), custom_call_target="tpu_custom_call" | custom-call | tf_op jit(solution)/shard_map/normal_equations/pallas_call | solution.py:657
  99.4 0.0 copy-start.1
  99.4 0.0 copy-start
  99.4 3.2 %copy.10 = f32[512,1024]{1,0:T(8,128)} copy(f32[512,1024]{1,0:T(8,128)} %get-tuple-element.6) | data formatting | bytes 4194304
  102.6 0.0 copy-done.1
  102.6 0.6 copy.11
  103.2 0.0 copy-done
  103.2 0.6 copy.12
Async XLA Ops:
  99.4 3.2 %copy-start.1 = (f32[1024]{0:T(1024)S(1)}, f32[1024]{0:T(1024)}, u32[]{:S(2)}) copy-start(f32[1024]{0:T(1024)} %get-tuple-element.7) | copy-start | bytes 12292
  99.4 3.8 %copy-start = (f32[640]{0:T(1024)S(1)}, f32[640]{0:T(1024)}, u32[]{:S(2)}) copy-start(f32[640]{0:T(1024)} %get-tuple-element.8) | copy-start | bytes 7684

commit v7 on v6

--- a/solution.py
+++ b/solution.py
@@ -285,8 +285,8 @@
     def multiply(dy, m, q, e=None):
         role = (near + dy) % 4
 
-        def chunk(c, _):
-            at = pl.ds(pl.multiple_of(c * 256, 256), 256)
+        def form():
+            at = pl.ds(0, 512)
             value = jnp.dot(rows[dy, m, span(e)], cols[q // 2, q % 2, :, at], preferred_element_type=F32)
 
             @pl.when(role == 0)
@@ -297,9 +297,7 @@
             def _():
                 part[role - 1, m, q, span(e), at] = value.astype(BF16)
 
-            return 0
-
-        lax.fori_loop(0, 2, chunk, 0)
+        form()
 
         if q % 2 == 1 and e == 1:
             return

time: 104 us -> 103 us (level)
  Pallas kernels: 98.8 us -> 97.4 us
    pallas_call x1, Pallas kernels: 98.8 us -> 97.4 us  [per_device(): pl.pallas_call(functools.partial(kernel, 1.0 / total_rows, 1.0 / math.sqr...]
where the time goes in v7:
time: 103 us; the launch traced here: 102 us
  Pallas kernels  97.4 us (95%)
  local copies, waits for them, and re-layouts  4.36 us (4%)
    pallas_call x1, Pallas kernels, per_device(): pl.pallas_call(functools.partial(kernel, 1.0 / total_rows, 1.0 / math.sqr...  97.4 us
    unnamed x7, local copies, waits for them, and re-layouts  4.36 us

profile of v7, /device:TPU:34, one launch (start us, length us, event | category | flops | bytes accessed | tf_op | source)
XLA Modules:
  0.0 102.4 jit_solution(4716377512635474310)
XLA Ops:
  0.6 97.4 %normal_equations.1 = (f32[512,1024]{1,0:T(8,128)}, f32[1024]{0:T(1024)}, f32[640]{0:T(1024)}) custom-call(bf16[640,1024]{1,0:T(8,128)(2,1)} %design_hbm.1, bf16[640]{0:T(1024)(128)(2,1)} %observed.1, f32[640]{0:T(1024)} %weight.1, f32[7]{0:T(128)} %taps.1), custom_call_target="tpu_custom_call" | custom-call | tf_op jit(solution)/shard_map/normal_equations/pallas_call | solution.py:655
  98.0 0.0 copy-start.1
  98.0 0.0 copy-start
  98.0 3.2 %copy.10 = f32[512,1024]{1,0:T(8,128)} copy(f32[512,1024]{1,0:T(8,128)} %get-tuple-element.6) | data formatting | bytes 4194304
  101.2 0.0 copy-done.1
  101.2 0.6 copy.11
  101.8 0.0 copy-done
  101.8 0.6 copy.12
Async XLA Ops:
  98.0 3.2 %copy-start.1 = (f32[1024]{0:T(1024)S(1)}, f32[1024]{0:T(1024)}, u32[]{:S(2)}) copy-start(f32[1024]{0:T(1024)} %get-tuple-element.7) | copy-start | bytes 12292
  98.0 3.8 %copy-start = (f32[640]{0:T(1024)S(1)}, f32[640]{0:T(1024)}, u32[]{:S(2)}) copy-start(f32[640]{0:T(1024)} %get-tuple-element.8) | copy-start | bytes 7684

commit v8 on v7

--- a/solution.py
+++ b/solution.py
@@ -549,9 +549,9 @@
     def _():
         pass_over(0)
 
-    keep_near(0)
     last_sums(1, (near % 2) == 1)
     late_sums((near % 2) == 1)
+    keep_near(0)
     add_on(0)
     pass_over(1, 0)
     hand_on(0)

time: 103 us -> 103 us (level)
  no operation moved by 1% of the time
where the time goes in v8:
time: 103 us; the launch traced here: 102 us
  Pallas kernels  97.4 us (95%)
  local copies, waits for them, and re-layouts  4.36 us (4%)
    pallas_call x1, Pallas kernels, per_device(): pl.pallas_call(functools.partial(kernel, 1.0 / total_rows, 1.0 / math.sqr...  97.4 us
    unnamed x7, local copies, waits for them, and re-layouts  4.36 us

profile of v8, /device:TPU:34, one launch (start us, length us, event | category | flops | bytes accessed | tf_op | source)
XLA Modules:
  0.0 102.4 jit_solution(2705017827403040124)
XLA Ops:
  0.6 97.4 %normal_equations.1 = (f32[512,1024]{1,0:T(8,128)}, f32[1024]{0:T(1024)}, f32[640]{0:T(1024)}) custom-call(bf16[640,1024]{1,0:T(8,128)(2,1)} %design_hbm.1, bf16[640]{0:T(1024)(128)(2,1)} %observed.1, f32[640]{0:T(1024)} %weight.1, f32[7]{0:T(128)} %taps.1), custom_call_target="tpu_custom_call" | custom-call | tf_op jit(solution)/shard_map/normal_equations/pallas_call | solution.py:655
  98.0 0.0 copy-start.1
  98.0 0.0 copy-start
  98.0 3.2 %copy.10 = f32[512,1024]{1,0:T(8,128)} copy(f32[512,1024]{1,0:T(8,128)} %get-tuple-element.6) | data formatting | bytes 4194304
  101.2 0.0 copy-done.1
  101.2 0.6 copy.11
  101.8 0.0 copy-done
  101.8 0.6 copy.12
Async XLA Ops:
  98.0 3.2 %copy-start.1 = (f32[1024]{0:T(1024)S(1)}, f32[1024]{0:T(1024)}, u32[]{:S(2)}) copy-start(f32[1024]{0:T(1024)} %get-tuple-element.7) | copy-start | bytes 12292
  98.0 3.8 %copy-start = (f32[640]{0:T(1024)S(1)}, f32[640]{0:T(1024)}, u32[]{:S(2)}) copy-start(f32[640]{0:T(1024)} %get-tuple-element.8) | copy-start | bytes 7684
